TPU v7x, 128 devices: a whole 4x4x4 slice. The times are simulated.
128 devices in a mesh: rep: 8 (over z_lo, x), shard: 16 (over z_hi, y, core).
Axes of the slice: x: 4, y: 4, z: 4 (z_hi: 2, z_lo: 2; z = z_hi * 2 + z_lo), core: 2. Of those that a mesh axis runs over, the one named last changes fastest.
Arguments:
- inputs: bfloat16 [16, 1024, 512], P('rep', 'shard'), may hold values from -6 to 6
- qkv_weight: bfloat16 [2, 512, 1536], P(None, 'shard'), as said below
- proj_weight: bfloat16 [2, 512, 512], P(None, 'shard'), as said below
- up_weight: bfloat16 [2, 512, 2048], P(None, 'shard'), may hold values from -0.25 to 0.25
- down_weight: bfloat16 [2, 2048, 512], P(None, 'shard'), may hold values from -0.125 to 0.125
- bias_rows: bfloat16 [2, 3, 512], P(None, None, 'shard'), may hold values from -2 to 2
- norm_gain: bfloat16 [2, 2, 512], P(None, None, 'shard'), may hold values from 0.5 to 1.5
- norm_shift: bfloat16 [2, 2, 512], P(None, None, 'shard'), may hold values from -2 to 2
- up_bias: bfloat16 [2, 2048], P(None, 'shard'), may hold values from -2 to 2
- cotangent: bfloat16 [16, 1024, 512], P('rep', 'shard'), may hold values from -6 to 6
Outputs:
- outputs: bfloat16 [16, 1024, 512], P('rep', 'shard')
- input_grad: float32 [16, 1024, 512], P('rep', 'shard')
- qkv_grad: float32 [2, 512, 1536], P(None, 'shard')
- proj_grad: float32 [2, 512, 512], P(None, 'shard')
- up_grad: float32 [2, 512, 2048], P(None, 'shard')
- down_grad: float32 [2, 2048, 512], P(None, 'shard')
- bias_grad: float32 [2, 3, 512], P(None, None, 'shard')
- gain_grad: float32 [2, 2, 512], P(None, None, 'shard')
- shift_grad: float32 [2, 2, 512], P(None, None, 'shard')
- up_bias_grad: float32 [2, 2048], P(None, 'shard')
Inputs may be any that keep to these rules, and one draw needn't show every extreme that they name: `qkv_weight`: entries of a normal law of deviation 512^-0.5, clipped at four deviations. `proj_weight`: entries of a normal law of deviation max(2, 1)^-0.5, clipped at four deviations.
All inputs are finite; a program needn't handle non-finite values.
Results may differ from a plain program's by a relative error of at most 0.022.
Values may be sent and summed in bfloat16 or wider, within the bound.
A program may use at most 128 MiB of HBM per device.

v0:
```python
from functools import partial

import jax
import jax.numpy as jnp
from jax import lax
from jax.sharding import PartitionSpec as P

H = 8


def layer_norm(values, gain, shift):
    center = values - jnp.mean(values, axis=-1, keepdims=True)
    spread = jnp.mean(center * center, axis=-1, keepdims=True)
    return center * lax.rsqrt(spread + 1e-06) * gain + shift


def left_product(first_op, second_op):
    return lax.dot_general(
        first_op, second_op, (((0,), (0,)), ((), ())), preferred_element_type=jnp.float32
    )


def right_product(first_op, second_op):
    return lax.dot_general(
        first_op, second_op, (((1,), (1,)), ((), ())), preferred_element_type=jnp.float32
    )


def attn_scores(queries, keys_all, scale):
    return (
        jnp.einsum("sqhd,skhd->shqk", queries, keys_all, preferred_element_type=jnp.float32) * scale
    )


def shards(
    inputs,
    qkv_weight,
    proj_weight,
    up_weight,
    down_weight,
    bias_rows,
    norm_gain,
    norm_shift,
    up_bias,
    cotangent,
):
    seqs_dev, local_len, width = inputs.shape
    heads = H
    head_dim = width // heads
    scale = head_dim ** (-0.5)
    layers = qkv_weight.shape[0]
    gelu_exact = partial(jax.nn.gelu, approximate=False)
    hidden = inputs.reshape(-1, width).astype(jnp.float32)
    saved = []
    for layer_at in range(layers):
        weights = (
            lax.all_gather(qkv_weight[layer_at], "shard", axis=0, tiled=True),
            lax.all_gather(proj_weight[layer_at], "shard", axis=0, tiled=True),
            lax.all_gather(up_weight[layer_at], "shard", axis=0, tiled=True),
            lax.all_gather(down_weight[layer_at], "shard", axis=0, tiled=True),
            lax.all_gather(bias_rows[layer_at], "shard", axis=1, tiled=True),
            lax.all_gather(norm_gain[layer_at], "shard", axis=1, tiled=True),
            lax.all_gather(norm_shift[layer_at], "shard", axis=1, tiled=True),
            lax.all_gather(up_bias[layer_at], "shard", axis=0, tiled=True),
        )
        qkv_w, proj_w, up_w, down_w, biases, gains, shifts, up_b = weights
        biases = biases.astype(jnp.float32)
        gains = gains.astype(jnp.float32)
        shifts = shifts.astype(jnp.float32)
        up_b = up_b.astype(jnp.float32)
        source = hidden.astype(jnp.bfloat16)
        bias_all = jnp.concatenate(
            [jnp.zeros_like(biases[0]), jnp.zeros_like(biases[0]), biases[0]]
        )
        joined = (jnp.dot(source, qkv_w, preferred_element_type=jnp.float32) + bias_all).astype(
            jnp.bfloat16
        )
        shaped = joined.reshape(seqs_dev, local_len, 3, heads, head_dim)
        queries = shaped[:, :, 0]
        keys_all, values_all = (
            lax.all_gather(shaped[:, :, 1], "shard", axis=1, tiled=True),
            lax.all_gather(shaped[:, :, 2], "shard", axis=1, tiled=True),
        )
        scores = attn_scores(queries, keys_all, scale)
        top = jnp.max(scores, axis=-1, keepdims=True)
        expo = jnp.exp(scores - top)
        total = jnp.sum(expo, axis=-1, keepdims=True)
        probs = expo / total
        log_total = top + jnp.log(total)
        context = jnp.einsum(
            "shqk,skhd->sqhd",
            probs.astype(jnp.bfloat16),
            values_all,
            preferred_element_type=jnp.float32,
        )
        context = context.reshape(-1, width).astype(jnp.bfloat16)
        first = hidden + jnp.dot(context, proj_w, preferred_element_type=jnp.float32) + biases[1]
        middle = layer_norm(first, gains[0], shifts[0])
        mid_low = middle.astype(jnp.bfloat16)
        upper = jnp.dot(mid_low, up_w, preferred_element_type=jnp.float32) + up_b
        active = gelu_exact(upper).astype(jnp.bfloat16)
        second = middle + jnp.dot(active, down_w, preferred_element_type=jnp.float32) + biases[2]
        saved.append(
            (
                source,
                queries,
                keys_all,
                values_all,
                log_total,
                context,
                first,
                mid_low,
                upper,
                active,
                second,
                weights,
            )
        )
        hidden = layer_norm(second, gains[1], shifts[1])
    outputs = hidden.reshape(inputs.shape).astype(jnp.bfloat16)
    grad = cotangent.reshape(-1, width).astype(jnp.float32)
    shard_grads = []
    for layer_at in reversed(range(layers)):
        (
            source,
            queries,
            keys_all,
            values_all,
            log_total,
            context,
            first,
            mid_low,
            upper,
            active,
            second,
            kept_weights,
        ) = saved[layer_at]
        weights = (
            lax.all_gather(qkv_weight[layer_at], "shard", axis=0, tiled=True),
            lax.all_gather(proj_weight[layer_at], "shard", axis=0, tiled=True),
            lax.all_gather(up_weight[layer_at], "shard", axis=0, tiled=True),
            lax.all_gather(down_weight[layer_at], "shard", axis=0, tiled=True),
            lax.all_gather(bias_rows[layer_at], "shard", axis=1, tiled=True),
            lax.all_gather(norm_gain[layer_at], "shard", axis=1, tiled=True),
            lax.all_gather(norm_shift[layer_at], "shard", axis=1, tiled=True),
            lax.all_gather(up_bias[layer_at], "shard", axis=0, tiled=True),
        )
        qkv_w, proj_w, up_w, down_w, biases, gains, shifts, up_b = weights
        gains = gains.astype(jnp.float32)
        shifts = shifts.astype(jnp.float32)
        _, norm_pull_two = jax.vjp(layer_norm, second, gains[1], shifts[1])
        d_second, d_gain_two, d_shift_two = norm_pull_two(grad)
        d_branch_two = d_second.astype(jnp.bfloat16)
        d_down_bias = jnp.sum(d_branch_two.astype(jnp.float32), axis=0)
        d_down = left_product(active, d_branch_two)
        d_active = right_product(d_branch_two, down_w)
        _, gelu_pull = jax.vjp(gelu_exact, upper)
        d_upper = gelu_pull(d_active)[0].astype(jnp.bfloat16)
        d_up_bias = jnp.sum(d_upper.astype(jnp.float32), axis=0)
        d_up = left_product(mid_low, d_upper)
        d_middle = d_second + right_product(d_upper, up_w)
        _, norm_pull_one = jax.vjp(layer_norm, first, gains[0], shifts[0])
        d_first, d_gain_one, d_shift_one = norm_pull_one(d_middle)
        d_branch = d_first.astype(jnp.bfloat16)
        d_proj_bias = jnp.sum(d_branch.astype(jnp.float32), axis=0)
        d_proj = left_product(context, d_branch)
        d_context = (
            right_product(d_branch, proj_w)
            .astype(jnp.bfloat16)
            .reshape(seqs_dev, local_len, heads, head_dim)
        )
        probs = jnp.exp(attn_scores(queries, keys_all, scale) - log_total)
        d_probs = jnp.einsum(
            "sqhd,skhd->shqk", d_context, values_all, preferred_element_type=jnp.float32
        )
        d_values_all = jnp.einsum(
            "shqk,sqhd->skhd",
            probs.astype(jnp.bfloat16),
            d_context,
            preferred_element_type=jnp.float32,
        )
        row_dot = jnp.sum(probs * d_probs, axis=-1, keepdims=True)
        d_scores = (probs * (d_probs - row_dot)).astype(jnp.bfloat16)
        d_queries = (
            jnp.einsum("shqk,skhd->sqhd", d_scores, keys_all, preferred_element_type=jnp.float32)
            * scale
        )
        d_keys_all = (
            jnp.einsum("shqk,sqhd->skhd", d_scores, queries, preferred_element_type=jnp.float32)
            * scale
        )
        d_keys, d_values = (
            lax.psum_scatter(
                d_keys_all.astype(jnp.bfloat16), "shard", scatter_dimension=1, tiled=True
            ).astype(jnp.float32),
            lax.psum_scatter(
                d_values_all.astype(jnp.bfloat16), "shard", scatter_dimension=1, tiled=True
            ).astype(jnp.float32),
        )
        d_joined = (
            jnp.stack([d_queries, d_keys, d_values], axis=2)
            .reshape(-1, 3 * width)
            .astype(jnp.bfloat16)
        )
        d_value_bias = jnp.sum(d_joined[:, 2 * width :].astype(jnp.float32), axis=0)
        d_qkv = left_product(source, d_joined)
        grad = d_first + right_product(d_joined, qkv_w)
        d_biases = jnp.stack([d_value_bias, d_proj_bias, d_down_bias])
        d_gains = jnp.stack([d_gain_one, d_gain_two])
        d_shifts = jnp.stack([d_shift_one, d_shift_two])
        g_qkv, g_proj, g_up, g_down, g_biases, g_gains, g_shifts, g_up_bias = (
            lax.psum_scatter(
                d_qkv.astype(jnp.bfloat16), "shard", scatter_dimension=0, tiled=True
            ).astype(jnp.float32),
            lax.psum_scatter(
                d_proj.astype(jnp.bfloat16), "shard", scatter_dimension=0, tiled=True
            ).astype(jnp.float32),
            lax.psum_scatter(
                d_up.astype(jnp.bfloat16), "shard", scatter_dimension=0, tiled=True
            ).astype(jnp.float32),
            lax.psum_scatter(
                d_down.astype(jnp.bfloat16), "shard", scatter_dimension=0, tiled=True
            ).astype(jnp.float32),
            lax.psum_scatter(
                d_biases.astype(jnp.bfloat16), "shard", scatter_dimension=1, tiled=True
            ).astype(jnp.float32),
            lax.psum_scatter(
                d_gains.astype(jnp.bfloat16), "shard", scatter_dimension=1, tiled=True
            ).astype(jnp.float32),
            lax.psum_scatter(
                d_shifts.astype(jnp.bfloat16), "shard", scatter_dimension=1, tiled=True
            ).astype(jnp.float32),
            lax.psum_scatter(
                d_up_bias.astype(jnp.bfloat16), "shard", scatter_dimension=0, tiled=True
            ).astype(jnp.float32),
        )
        g_qkv, g_proj, g_up, g_down, g_biases, g_gains, g_shifts, g_up_bias = (
            lax.psum(g_qkv.astype(jnp.bfloat16), "rep").astype(jnp.float32),
            lax.psum(g_proj.astype(jnp.bfloat16), "rep").astype(jnp.float32),
            lax.psum(g_up.astype(jnp.bfloat16), "rep").astype(jnp.float32),
            lax.psum(g_down.astype(jnp.bfloat16), "rep").astype(jnp.float32),
            lax.psum(g_biases.astype(jnp.bfloat16), "rep").astype(jnp.float32),
            lax.psum(g_gains.astype(jnp.bfloat16), "rep").astype(jnp.float32),
            lax.psum(g_shifts.astype(jnp.bfloat16), "rep").astype(jnp.float32),
            lax.psum(g_up_bias.astype(jnp.bfloat16), "rep").astype(jnp.float32),
        )
        shard_grads.insert(0, (g_qkv, g_proj, g_up, g_down, g_biases, g_gains, g_shifts, g_up_bias))
    input_grad = grad.reshape(inputs.shape)
    s_qkv, s_proj, s_up, s_down, s_biases, s_gains, s_shifts, s_up_bias = tuple(
        (jnp.stack([entry[index] for entry in shard_grads]) for index in range(8))
    )
    return (
        outputs,
        input_grad,
        s_qkv,
        s_proj,
        s_up,
        s_down,
        s_biases,
        s_gains,
        s_shifts,
        s_up_bias,
    )


def solution(mesh):
    placed = (
        P("rep", "shard", None),
        P(None, "shard", None),
        P(None, "shard", None),
        P(None, "shard", None),
        P(None, "shard", None),
        P(None, None, "shard"),
        P(None, None, "shard"),
        P(None, None, "shard"),
        P(None, "shard"),
        P("rep", "shard", None),
    )
    return jax.shard_map(
        shards,
        mesh=mesh,
        in_specs=placed,
        out_specs=(
            P("rep", "shard", None),
            P("rep", "shard", None),
            P(None, "shard", None),
            P(None, "shard", None),
            P(None, "shard", None),
            P(None, "shard", None),
            P(None, None, "shard"),
            P(None, None, "shard"),
            P(None, None, "shard"),
            P(None, "shard"),
        ),
        check_vma=False,
    )
```

profile of v0, /device:TPU:0, one launch (start us, length us, event | category | flops | bytes accessed | tf_op | source)
XLA Modules:
  0.0 2064.8 jit_solution(1429953635220243129)
XLA Ops:
  9.8 26.0 %all-gather.1 = bf16[1,3,512]{1,0,2:T(2,128)(2,1)S(1)} all-gather(bf16[1,3,32]{1,0,2:T(2,128)(2,1)S(1)} %copy.140), channel_id=3, replica_groups=mesh['rep'=8,'shard'=16] {'shard'}, dimensions={2}, use_global_device_ids=true | all-gather | bytes 3264 | tf_op jit(solution)/shard_map/all_gather | solution.py:61
  36.1 4.8 slice_reduce_fusion.9
  41.0 19.4 all-gather.31.cloned.1.call-done
  66.8 21.1 %all-gather.8 = bf16[1,2048]{1,0:T(2,128)(2,1)S(1)} all-gather(bf16[1,128]{1,0:T(2,128)(2,1)S(1)} %get-tuple-element.134), channel_id=10, replica_groups=mesh['rep'=8,'shard'=16] {'shard'}, dimensions={1}, use_global_device_ids=true | all-gather | bytes 4352 | tf_op jit(solution)/shard_map/all_gather | solution.py:64
  88.2 20.2 all-gather.5
  111.5 21.3 %all-gather.6 = bf16[1,2,512]{1,0,2:T(2,128)(2,1)S(1)} all-gather(bf16[1,2,32]{1,0,2:T(2,128)(2,1)S(1)} %copy.145), channel_id=8, replica_groups=mesh['rep'=8,'shard'=16] {'shard'}, dimensions={2}, use_global_device_ids=true | all-gather | bytes 2176 | tf_op jit(solution)/shard_map/all_gather | solution.py:63
  135.8 20.8 %all-gather.11 = bf16[1,3,512]{1,0,2:T(2,128)(2,1)S(1)} all-gather(bf16[1,3,32]{1,0,2:T(2,128)(2,1)S(1)} %copy.146), channel_id=13, replica_groups=mesh['rep'=8,'shard'=16] {'shard'}, dimensions={2}, use_global_device_ids=true | all-gather | bytes 3264 | tf_op jit(solution)/shard_map/all_gather | solution.py:61
  156.8 5.4 slice_reduce_fusion.2
  162.2 22.7 %all-gather.4 = bf16[1,512,512]{2,1,0:T(8,128)(2,1)S(1)} all-gather(bf16[1,32,512]{2,1,0:T(8,128)(2,1)S(1)} %get-tuple-element.127), channel_id=6, replica_groups=mesh['rep'=8,'shard'=16] {'shard'}, dimensions={1}, use_global_device_ids=true | all-gather | bytes 557056 | tf_op jit(solution)/shard_map/all_gather | solution.py:58
  185.0 4.7 copy.89
  193.3 5.5 copy.86
  198.8 4.1 fusion.107
  203.9 23.5 %all-gather.37.cloned.1.call-done = bf16[1,512,2048]{2,1,0:T(8,128)(2,1)} async-done(((bf16[1,32,2048]{2,1,0:T(8,128)(2,1)}), bf16[1,512,2048]{2,1,0:T(8,128)(2,1)}) %all-gather.37.cloned.1.call-update) | async-done | bytes 2097168 | tf_op jit(solution)/shard_map/all_gather | solution.py:59
  227.4 5.5 multiply_convert_fusion.5
  233.0 44.4 %all-gather.39.cloned.1.call-done = bf16[1,2048,512]{2,1,0:T(8,128)(2,1)} async-done(((bf16[1,128,512]{2,1,0:T(8,128)(2,1)}), bf16[1,2048,512]{2,1,0:T(8,128)(2,1)}) %all-gather.39.cloned.1.call-update) | async-done | bytes 2097168 | tf_op jit(solution)/shard_map/all_gather | solution.py:60
  279.8 45.4 %all-gather.41.cloned.1.call-done = bf16[1,512,1536]{2,1,0:T(8,128)(2,1)} async-done(((bf16[1,32,1536]{2,1,0:T(8,128)(2,1)}), bf16[1,512,1536]{2,1,0:T(8,128)(2,1)}) %all-gather.41.cloned.1.call-update) | async-done | bytes 1572880 | tf_op jit(solution)/shard_map/all_gather | solution.py:57
  334.4 21.1 %all-gather.18 = bf16[1,2048]{1,0:T(2,128)(2,1)S(1)} all-gather(bf16[1,128]{1,0:T(2,128)(2,1)S(1)} %get-tuple-element.135), channel_id=20, replica_groups=mesh['rep'=8,'shard'=16] {'shard'}, dimensions={1}, use_global_device_ids=true | all-gather | bytes 4352 | tf_op jit(solution)/shard_map/all_gather | solution.py:64
  356.2 20.2 all-gather.15
  376.7 21.3 %all-gather.16 = bf16[1,2,512]{1,0,2:T(2,128)(2,1)S(1)} all-gather(bf16[1,2,32]{1,0,2:T(2,128)(2,1)S(1)} %copy.151), channel_id=18, replica_groups=mesh['rep'=8,'shard'=16] {'shard'}, dimensions={2}, use_global_device_ids=true | all-gather | bytes 2176 | tf_op jit(solution)/shard_map/all_gather | solution.py:63
  398.3 3.3 slice_reduce_fusion.1
  401.6 3.3 slice_reduce_fusion
  405.0 21.4 %all-gather.14 = bf16[1,512,512]{2,1,0:T(8,128)(2,1)S(1)} all-gather(bf16[1,32,512]{2,1,0:T(8,128)(2,1)S(1)} %get-tuple-element.126), channel_id=16, replica_groups=mesh['rep'=8,'shard'=16] {'shard'}, dimensions={1}, use_global_device_ids=true | all-gather | bytes 557056 | tf_op jit(solution)/shard_map/all_gather | solution.py:58
  426.4 5.5 copy.95
  431.8 13.7 all-gather.45.cloned.1.call-done
  445.5 5.5 copy.98
  463.2 32.4 %all-gather.47.cloned.1.call-done = bf16[1,512,2048]{2,1,0:T(8,128)(2,1)} async-done(((bf16[1,32,2048]{2,1,0:T(8,128)(2,1)}), bf16[1,512,2048]{2,1,0:T(8,128)(2,1)}) %all-gather.47.cloned.1.call-update) | async-done | bytes 2097168 | tf_op jit(solution)/shard_map/all_gather | solution.py:59
  495.6 5.7 multiply_convert_fusion.4
  501.3 43.8 %all-gather.49.cloned.1.call-done = bf16[1,2048,512]{2,1,0:T(8,128)(2,1)} async-done(((bf16[1,128,512]{2,1,0:T(8,128)(2,1)}), bf16[1,2048,512]{2,1,0:T(8,128)(2,1)}) %all-gather.49.cloned.1.call-update) | async-done | bytes 2097168 | tf_op jit(solution)/shard_map/all_gather | solution.py:60
  556.0 4.5 multiply_reduce_fusion.1
  565.1 6.6 copy.116
  571.7 6.5 reshape.293
  578.3 4.5 convert_bitcast_fusion.1
  582.8 6.3 copy.118
  589.1 6.6 reshape.295
  596.4 3.0 fusion.75
  599.4 48.5 %reduce-scatter.55.cloned.1.call-done = bf16[64,1024]{1,0:T(8,128)(2,1)} async-done(((bf16[1024,1024]{1,0:T(8,128)(2,1)}), bf16[64,1024]{1,0:T(8,128)(2,1)}) %reduce-scatter.55.cloned.1.call-update) | async-done | bytes 131088
  650.0 71.6 %reduce-scatter.57.cloned.1.call-done = bf16[64,1024]{1,0:T(8,128)(2,1)} async-done(((bf16[1024,1024]{1,0:T(8,128)(2,1)}), bf16[64,1024]{1,0:T(8,128)(2,1)}) %reduce-scatter.57.cloned.1.call-update) | async-done | bytes 131088
  745.0 4.6 multiply_reduce_fusion
  754.2 6.2 copy.120
  760.5 6.5 reshape.297
  767.1 4.6 convert_bitcast_fusion
  771.6 6.2 copy.122
  777.8 6.6 reshape.299
  792.3 3.0 fusion.60
  802.0 35.1 %reduce-scatter.59.cloned.1.call-done = bf16[64,1024]{1,0:T(8,128)(2,1)} async-done(((bf16[1024,1024]{1,0:T(8,128)(2,1)}), bf16[64,1024]{1,0:T(8,128)(2,1)}) %reduce-scatter.59.cloned.1.call-update) | async-done | bytes 131088
  838.5 72.4 %reduce-scatter.61.cloned.1.call-done = bf16[64,1024]{1,0:T(8,128)(2,1)} async-done(((bf16[1024,1024]{1,0:T(8,128)(2,1)}), bf16[64,1024]{1,0:T(8,128)(2,1)}) %reduce-scatter.61.cloned.1.call-update) | async-done | bytes 131088
  922.8 3.3 convolution_convert_fusion.2
  934.1 44.3 %reduce-scatter.77.cloned.1.call-done = bf16[32,2]{1,0:T(8,128)(2,1)} async-done(((bf16[512,2]{1,0:T(8,128)(2,1)}), bf16[32,2]{1,0:T(8,128)(2,1)}) %reduce-scatter.77.cloned.1.call-update) | async-done | bytes 144
  979.6 67.2 %reduce-scatter.73.cloned.1.call-done = bf16[32,2]{1,0:T(8,128)(2,1)} async-done(((bf16[512,2]{1,0:T(8,128)(2,1)}), bf16[32,2]{1,0:T(8,128)(2,1)}) %reduce-scatter.73.cloned.1.call-update) | async-done | bytes 144
  1048.1 33.7 %all-reduce.4 = (bf16[2048]{0:T(1024)(128)(2,1)S(1)}, bf16[2048]{0:T(1024)(128)(2,1)S(1)}) all-reduce(bf16[2048]{0:T(1024)(128)(2,1)S(1)} %copy-done.86, bf16[2048]{0:T(1024)(128)(2,1)S(1)} %copy-done.87), channel_id=41, replica_groups=mesh['rep'=8,'shard'=16] {'shard'}, use_global_device_ids=true, to_apply=%region_72.0.clone | all-reduce | flops 4096 | bytes 16384
  1082.5 31.9 %reduce-scatter.75.cloned.1.call-done = bf16[32,2]{1,0:T(8,128)(2,1)} async-done(((bf16[512,2]{1,0:T(8,128)(2,1)}), bf16[32,2]{1,0:T(8,128)(2,1)}) %reduce-scatter.75.cloned.1.call-update) | async-done | bytes 144
  1115.6 66.7 %reduce-scatter.71.cloned.1.call-done = bf16[32,2]{1,0:T(8,128)(2,1)} async-done(((bf16[512,2]{1,0:T(8,128)(2,1)}), bf16[32,2]{1,0:T(8,128)(2,1)}) %reduce-scatter.71.cloned.1.call-update) | async-done | bytes 144
  1183.6 66.9 %reduce-scatter.69.cloned.1.call-done = bf16[32,3]{1,0:T(8,128)(2,1)} async-done(((bf16[512,3]{1,0:T(8,128)(2,1)}), bf16[32,3]{1,0:T(8,128)(2,1)}) %reduce-scatter.69.cloned.1.call-update) | async-done | bytes 208
  1251.9 67.2 %reduce-scatter.67.cloned.1.call-done = bf16[32,3]{1,0:T(8,128)(2,1)} async-done(((bf16[512,3]{1,0:T(8,128)(2,1)}), bf16[32,3]{1,0:T(8,128)(2,1)}) %reduce-scatter.67.cloned.1.call-update) | async-done | bytes 208
  1320.4 67.5 %reduce-scatter.45.cloned.1.call-done = bf16[32,512]{1,0:T(8,128)(2,1)} async-done(((bf16[512,512]{1,0:T(8,128)(2,1)}), bf16[32,512]{1,0:T(8,128)(2,1)}) %reduce-scatter.45.cloned.1.call-update) | async-done | bytes 32784 | tf_op jit(solution)/shard_map/reduce_scatter | solution.py:215
  1387.8 68.7 %reduce-scatter.43.cloned.1.call-done = bf16[32,512]{1,0:T(8,128)(2,1)} async-done(((bf16[512,512]{1,0:T(8,128)(2,1)}), bf16[32,512]{1,0:T(8,128)(2,1)}) %reduce-scatter.43.cloned.1.call-update) | async-done | bytes 32784 | tf_op jit(solution)/shard_map/reduce_scatter | solution.py:215
  1456.6 71.6 %reduce-scatter.65.cloned.1.call-done = bf16[32,1536]{1,0:T(8,128)(2,1)} async-done(((bf16[512,1536]{1,0:T(8,128)(2,1)}), bf16[32,1536]{1,0:T(8,128)(2,1)}) %reduce-scatter.65.cloned.1.call-update) | async-done | bytes 98320
  1530.0 69.8 %reduce-scatter.63.cloned.1.call-done = bf16[32,1536]{1,0:T(8,128)(2,1)} async-done(((bf16[512,1536]{1,0:T(8,128)(2,1)}), bf16[32,1536]{1,0:T(8,128)(2,1)}) %reduce-scatter.63.cloned.1.call-update) | async-done | bytes 98320
  1601.6 72.0 %reduce-scatter.49.cloned.1.call-done = bf16[32,2048]{1,0:T(8,128)(2,1)} async-done(((bf16[512,2048]{1,0:T(8,128)(2,1)}), bf16[32,2048]{1,0:T(8,128)(2,1)}) %reduce-scatter.49.cloned.1.call-update) | async-done | bytes 131088 | tf_op jit(solution)/shard_map/reduce_scatter | solution.py:218
  1673.6 73.7 %reduce-scatter.53.cloned.1.call-done = bf16[128,512]{1,0:T(8,128)(2,1)} async-done(((bf16[2048,512]{1,0:T(8,128)(2,1)}), bf16[128,512]{1,0:T(8,128)(2,1)}) %reduce-scatter.53.cloned.1.call-update) | async-done | bytes 131088 | tf_op jit(solution)/shard_map/reduce_scatter | solution.py:221
  1747.3 73.7 %reduce-scatter.47.cloned.1.call-done = bf16[32,2048]{1,0:T(8,128)(2,1)} async-done(((bf16[512,2048]{1,0:T(8,128)(2,1)}), bf16[32,2048]{1,0:T(8,128)(2,1)}) %reduce-scatter.47.cloned.1.call-update) | async-done | bytes 131088 | tf_op jit(solution)/shard_map/reduce_scatter | solution.py:218
  1821.0 73.8 %reduce-scatter.51.cloned.1.call-done = bf16[128,512]{1,0:T(8,128)(2,1)} async-done(((bf16[2048,512]{1,0:T(8,128)(2,1)}), bf16[128,512]{1,0:T(8,128)(2,1)}) %reduce-scatter.51.cloned.1.call-update) | async-done | bytes 131088 | tf_op jit(solution)/shard_map/reduce_scatter | solution.py:221
  1896.2 72.4 %all-reduce.10.cloned.1.call-done = (bf16[1,32,512]{2,1,0:T(8,128)(2,1)}, bf16[1,32,512]{2,1,0:T(8,128)(2,1)}, bf16[1,3,32]{2,1,0:T(4,128)(2,1)}, bf16[1,3,32]{2...) async-done(((bf16[1,32,512]{2,1,0:T(8,128)(2,1)}, ...) | async-done | bytes 66960 | tf_op jit(solution)/shard_map/psum | solution.py:239
  1975.0 77.0 %all-reduce.12.cloned.1.call-done = (bf16[1,32,1536]{1,2,0:T(8,128)(2,1)}, bf16[1,32,1536]{1,2,0:T(8,128)(2,1)}, bf16[1,32,2048]{2,1,0:T(8,128)(2,1)}, bf16[1,32...) async-done(((bf16[1,32,1536]{1,2,0:T(8,128)(2,1)}, bf16[1,32,1536]{1,2,0:T(8,128)(2,1)}, bf16[1,32,2048]{2,1,0:T(8,128)(2,1)}, ...) | async-done | bytes 720912 | tf_op jit(solution)/shard_map/psum | solution.py:238
  (439 shorter events, 151.5 us)
Async XLA Ops:
  7.2 53.2 %copy-start.29 = (bf16[2,64,512]{2,1,0:T(8,128)(2,1)S(1)}, bf16[2,64,512]{2,1,0:T(8,128)(2,1)}, u32[]{:S(2)}) copy-start(bf16[2,64,512]{2,1,0:T(8,128)(2,1)} %param.10) | copy-start | bytes 393220
  7.2 53.2 %all-gather.31.cloned.1.call-start = ((), (), s32[]{:S(2)}) async-start(), calls=%async_computation.24 | async-start | bytes 1671168 | tf_op jit(solution)/shard_map/all_gather | solution.py:57
  8.9 176.1 %all-gather.35.cloned.1.call-start = ((), (), s32[]{:S(2)}) async-start(), calls=%async_computation.26 | async-start | bytes 4456448 | tf_op jit(solution)/shard_map/all_gather | solution.py:81
  62.7 25.5 %copy-start.48 = (bf16[2,32,512]{2,1,0:T(8,128)(2,1)S(1)}, bf16[2,32,512]{2,1,0:T(8,128)(2,1)}, u32[]{:S(2)}) copy-start(bf16[2,32,512]{2,1,0:T(8,128)(2,1)} %param.12) | copy-start | bytes 196612
  62.9 126.8 %copy-start.12 = (bf16[2,64,1,8,64]{4,3,2,1,0:T(8,128)(2,1)}, bf16[2,64,1,8,64]{4,3,2,1,0:T(8,128)(2,1)S(1)}, u32[]{:S(2)}) copy-start(bf16[2,64,1,8,64]{4,3,2,1,0:T(8,128)(2,1)S(1)} %get-tuple-element.118) | copy-start | bytes 393220
  63.7 129.6 %all-gather.33.cloned.1.call-start = ((), (), s32[]{:S(2)}) async-start(), calls=%async_computation.25 | async-start | bytes 4456448 | tf_op jit(solution)/shard_map/all_gather | solution.py:82
  64.5 162.9 %all-gather.37.cloned.1.call-start = ((), (), s32[]{:S(2)}) async-start(), calls=%async_computation.27 | async-start | bytes 2228224 | tf_op jit(solution)/shard_map/all_gather | solution.py:59
  65.3 212.1 %all-gather.39.cloned.1.call-start = ((), (), s32[]{:S(2)}) async-start(), calls=%async_computation.28 | async-start | bytes 2228224 | tf_op jit(solution)/shard_map/all_gather | solution.py:60
  66.1 259.1 %all-gather.41.cloned.1.call-start = ((), (), s32[]{:S(2)}) async-start(), calls=%async_computation.29 | async-start | bytes 1671168 | tf_op jit(solution)/shard_map/all_gather | solution.py:57
  66.7 359.7 %all-gather.43.cloned.1.call-start = ((), (), s32[]{:S(2)}) async-start(), calls=%async_computation.30 | async-start | bytes 4456448 | tf_op jit(solution)/shard_map/all_gather | solution.py:82
  111.5 165.9 %copy-start.49 = (f32[512]{0:T(512)}, f32[512]{0:T(512)S(1)}, u32[]{:S(2)}) copy-start(f32[512]{0:T(512)S(1)} %get-tuple-element.69) | copy-start | bytes 6148
  111.5 348.4 %copy-start.46 = (f32[512]{0:T(512)}, f32[512]{0:T(512)S(1)}, u32[]{:S(2)}) copy-start(f32[512]{0:T(512)S(1)} %get-tuple-element.68) | copy-start | bytes 6148
  135.8 141.7 %copy-start.60 = (f32[512]{0:T(512)}, f32[512]{0:T(512)S(1)}, u32[]{:S(2)}) copy-start(f32[512]{0:T(512)S(1)} %get-tuple-element.71) | copy-start | bytes 6148
  135.8 189.5 %copy-start.56 = (f32[512]{0:T(512)}, f32[512]{0:T(512)S(1)}, u32[]{:S(2)}) copy-start(f32[512]{0:T(512)S(1)} %get-tuple-element.70) | copy-start | bytes 6148
  185.0 18.4 copy-start.8
  193.3 5.5 copy-start.53
  203.3 24.1 %copy-start.34 = (bf16[128,512]{1,0:T(8,128)(2,1)}, bf16[128,512]{1,0:T(8,128)(2,1)S(1)}, u32[]{:S(2)}) copy-start(bf16[128,512]{1,0:T(8,128)(2,1)S(1)} %convert_element_type.280) | copy-start | bytes 393220
  203.7 73.8 %copy-start.69 = (f32[128]{0:T(128)}, f32[128]{0:T(128)S(1)}, u32[]{:S(2)}) copy-start(f32[128]{0:T(128)S(1)} %broadcast_multiply_fusion.3) | copy-start | bytes 1540
  203.9 29.1 %copy-start.94 = (f32[128]{0:T(128)}, f32[128]{0:T(128)S(1)}, u32[]{:S(2)}) copy-start(f32[128]{0:T(128)S(1)} %multiply_reduce_fusion.13) | copy-start | bytes 1540
  203.9 73.6 %copy-start.76 = (f32[128]{0:T(128)}, f32[128]{0:T(128)S(1)}, u32[]{:S(2)}) copy-start(f32[128]{0:T(128)S(1)} %fusion.137) | copy-start | bytes 1540
  233.0 94.9 %copy-start.20 = (bf16[128,2048]{1,0:T(8,128)(2,1)}, bf16[128,2048]{1,0:T(8,128)(2,1)S(1)}, u32[]{:S(2)}) copy-start(bf16[128,2048]{1,0:T(8,128)(2,1)S(1)} %get-tuple-element.111) | copy-start | bytes 1572868
  279.6 51.7 %copy-start.63 = (f32[128]{0:T(128)}, f32[128]{0:T(128)S(1)}, u32[]{:S(2)}) copy-start(f32[128]{0:T(128)S(1)} %broadcast_multiply_fusion.2) | copy-start | bytes 1540
  279.8 51.6 %copy-start.96 = (f32[128]{0:T(128)}, f32[128]{0:T(128)S(1)}, u32[]{:S(2)}) copy-start(f32[128]{0:T(128)S(1)} %multiply_reduce_fusion.12) | copy-start | bytes 1540
  279.8 51.6 %copy-start.66 = (f32[128]{0:T(128)}, f32[128]{0:T(128)S(1)}, u32[]{:S(2)}) copy-start(f32[128]{0:T(128)S(1)} %fusion.138) | copy-start | bytes 1540
  331.3 119.6 %copy-start.14 = (bf16[2,64,1,8,64]{4,3,2,1,0:T(8,128)(2,1)}, bf16[2,64,1,8,64]{4,3,2,1,0:T(8,128)(2,1)S(1)}, u32[]{:S(2)}) copy-start(bf16[2,64,1,8,64]{4,3,2,1,0:T(8,128)(2,1)S(1)} %get-tuple-element.115) | copy-start | bytes 393220
  332.2 113.4 %all-gather.45.cloned.1.call-start = ((), (), s32[]{:S(2)}) async-start(), calls=%async_computation.31 | async-start | bytes 4456448 | tf_op jit(solution)/shard_map/all_gather | solution.py:81
  333.0 162.6 %all-gather.47.cloned.1.call-start = ((), (), s32[]{:S(2)}) async-start(), calls=%async_computation.32 | async-start | bytes 2228224 | tf_op jit(solution)/shard_map/all_gather | solution.py:59
  333.7 211.3 %all-gather.49.cloned.1.call-start = ((), (), s32[]{:S(2)}) async-start(), calls=%async_computation.33 | async-start | bytes 2228224 | tf_op jit(solution)/shard_map/all_gather | solution.py:60
  334.3 313.6 %reduce-scatter.55.cloned.1.call-start = ((), (), s32[]{:S(2)}) async-start(), calls=%async_computation.34 | async-start | bytes 2228224
  459.8 41.5 %copy-start.26 = (bf16[128,512]{1,0:T(8,128)(2,1)}, bf16[128,512]{1,0:T(8,128)(2,1)S(1)}, u32[]{:S(2)}) copy-start(bf16[128,512]{1,0:T(8,128)(2,1)S(1)} %convert_element_type.292) | copy-start | bytes 393220
  545.1 4.8 copy-start.19
  545.1 4.8 copy-start.102
  578.2 143.4 %reduce-scatter.57.cloned.1.call-start = ((), (), s32[]{:S(2)}) async-start(), calls=%async_computation.35 | async-start | bytes 2228224
  595.7 241.4 %reduce-scatter.59.cloned.1.call-start = ((), (), s32[]{:S(2)}) async-start(), calls=%async_computation.36 | async-start | bytes 2228224
  723.7 6.3 copy-start.11
  723.7 6.4 copy-start.47
  723.7 6.4 copy-start.64
  767.0 143.8 %reduce-scatter.61.cloned.1.call-start = ((), (), s32[]{:S(2)}) async-start(), calls=%async_computation.37 | async-start | bytes 2228224
  784.4 193.9 %reduce-scatter.77.cloned.1.call-start = ((), (), s32[]{:S(2)}) async-start(), calls=%async_computation.45 | async-start | bytes 139264
  788.2 258.7 %reduce-scatter.73.cloned.1.call-start = ((), (), s32[]{:S(2)}) async-start(), calls=%async_computation.43 | async-start | bytes 139264
  791.6 322.7 %reduce-scatter.75.cloned.1.call-start = ((), (), s32[]{:S(2)}) async-start(), calls=%async_computation.44 | async-start | bytes 139264
  795.3 117.0 %copy-start.36 = (bf16[2,64,1,8,64]{1,4,3,0,2:T(8,128)(2,1)S(1)}, bf16[2,64,1,8,64]{1,4,3,0,2:T(8,128)(2,1)}, u32[]{:S(2)}) copy-start(bf16[2,64,1,8,64]{1,4,3,0,2:T(8,128)(2,1)} %fusion.60) | copy-start | bytes 393220
  796.2 386.1 %reduce-scatter.71.cloned.1.call-start = ((), (), s32[]{:S(2)}) async-start(), calls=%async_computation.42 | async-start | bytes 139264
  797.8 452.7 %reduce-scatter.69.cloned.1.call-start = ((), (), s32[]{:S(2)}) async-start(), calls=%async_computation.41 | async-start | bytes 139264
  801.7 517.3 %reduce-scatter.67.cloned.1.call-start = ((), (), s32[]{:S(2)}) async-start(), calls=%async_computation.40 | async-start | bytes 139264
  913.0 5.5 copy-start.58
  913.0 5.5 copy-start.65
  913.0 5.5 copy-start.68
  915.1 472.8 %reduce-scatter.45.cloned.1.call-start = ((), (), s32[]{:S(2)}) async-start(), calls=%async_computation.19 | async-start | bytes 557056 | tf_op jit(solution)/shard_map/reduce_scatter | solution.py:215
  917.2 539.3 %reduce-scatter.43.cloned.1.call-start = ((), (), s32[]{:S(2)}) async-start(), calls=%async_computation.18 | async-start | bytes 557056 | tf_op jit(solution)/shard_map/reduce_scatter | solution.py:215
  918.4 609.8 %reduce-scatter.65.cloned.1.call-start = ((), (), s32[]{:S(2)}) async-start(), calls=%async_computation.39 | async-start | bytes 1671168
  920.4 679.4 %reduce-scatter.63.cloned.1.call-start = ((), (), s32[]{:S(2)}) async-start(), calls=%async_computation.38 | async-start | bytes 1671168
  922.7 750.9 %reduce-scatter.49.cloned.1.call-start = ((), (), s32[]{:S(2)}) async-start(), calls=%async_computation.21 | async-start | bytes 2228224 | tf_op jit(solution)/shard_map/reduce_scatter | solution.py:218
  926.1 821.2 %reduce-scatter.53.cloned.1.call-start = ((), (), s32[]{:S(2)}) async-start(), calls=%async_computation.23 | async-start | bytes 2228224 | tf_op jit(solution)/shard_map/reduce_scatter | solution.py:221
  928.3 892.7 %reduce-scatter.47.cloned.1.call-start = ((), (), s32[]{:S(2)}) async-start(), calls=%async_computation.20 | async-start | bytes 2228224 | tf_op jit(solution)/shard_map/reduce_scatter | solution.py:218
  930.6 117.6 %copy-start.86 = (bf16[2048]{0:T(1024)(128)(2,1)S(1)}, bf16[2048]{0:T(1024)(128)(2,1)}, u32[]{:S(2)}) copy-start(bf16[2048]{0:T(1024)(128)(2,1)} %get-tuple-element.157) | copy-start | bytes 12292
  930.6 117.6 %copy-start.87 = (bf16[2048]{0:T(1024)(128)(2,1)S(1)}, bf16[2048]{0:T(1024)(128)(2,1)}, u32[]{:S(2)}) copy-start(bf16[2048]{0:T(1024)(128)(2,1)} %get-tuple-element.159) | copy-start | bytes 12292
  930.6 964.2 %reduce-scatter.51.cloned.1.call-start = ((), (), s32[]{:S(2)}) async-start(), calls=%async_computation.22 | async-start | bytes 2228224 | tf_op jit(solution)/shard_map/reduce_scatter | solution.py:221
  932.7 962.1 %copy-start.7 = (bf16[1,512,1536]{2,1,0:T(8,128)(2,1)S(1)}, bf16[1,512,1536]{2,1,0:T(8,128)(2,1)}, u32[]{:S(2)}) copy-start(bf16[1,512,1536]{2,1,0:T(8,128)(2,1)} %all-gather.31.cloned.1.call-done) | copy-start | bytes 4718596
  932.7 962.1 %copy-start.91 = (f32[128]{0:T(128)S(1)}, f32[128]{0:T(128)}, u32[]{:S(2)}) copy-start(f32[128]{0:T(128)} %copy-done.90) | copy-start | bytes 1540
  932.8 1035.8 %all-reduce.10.cloned.1.call-start = ((), (), s32[]{:S(2)}) async-start(), calls=%async_computation.46 | async-start | bytes 141312 | tf_op jit(solution)/shard_map/psum | solution.py:239
  1456.5 595.5 %all-reduce.12.cloned.1.call-start = ((), (), s32[]{:S(2)}) async-start(), calls=%async_computation.47 | async-start | bytes 2621440 | tf_op jit(solution)/shard_map/psum | solution.py:238
  2052.0 4.9 copy-start.43
  2052.0 4.9 copy-start.44
  (70 other events, 170.5 us)
Sparse Core Ops, SparseCore 0:
  11.0 49.3 all-gather.30
  63.8 54.7 all-gather.34
  121.6 55.7 all-gather.32
  180.3 47.0 all-gather.36
  230.3 47.0 all-gather.38
  279.7 45.4 all-gather.40
  332.3 54.9 all-gather.42
  390.3 55.1 all-gather.44
  448.5 47.0 all-gather.46
  497.9 47.0 all-gather.48
  578.4 69.4 reduce-scatter.54
  651.7 69.8 reduce-scatter.56
  767.1 69.9 reduce-scatter.58
  840.9 69.9 reduce-scatter.60
  914.4 63.8 reduce-scatter.76
  983.0 63.8 reduce-scatter.72
  1050.4 63.8 reduce-scatter.74
  1118.4 63.9 reduce-scatter.70
  1186.6 63.8 reduce-scatter.68
  1255.1 63.8 reduce-scatter.66
  1323.4 64.4 reduce-scatter.44
  1392.1 64.3 reduce-scatter.42
  1460.4 67.7 reduce-scatter.64
  1531.9 67.8 reduce-scatter.62
  1603.7 69.8 reduce-scatter.48
  1677.4 69.8 reduce-scatter.52
  1751.1 69.8 reduce-scatter.46
  1824.9 69.8 reduce-scatter.50
  1899.3 69.3 all-reduce.9
  1972.3 79.6 all-reduce.11
where the time goes:
time: 2080 us; the launch traced here: 2060 us
  waiting for transfers between devices  1520 us (73%)
  blocking collectives  250 us (12%)
  local copies, waits for them, and re-layouts  165 us (8%)
  matrix products  87 us (4%)
  other arithmetic  28.4 us (1%)
    unnamed x42, waiting for transfers between devices  715 us
    reduce_scatter x2, waiting for transfers between devices, shards(): lax.psum_scatter(d_down.astype(jnp.bfloat16), 'shard', scatter_dimension=...  148 us
    reduce_scatter x2, waiting for transfers between devices, shards(): lax.psum_scatter(d_up.astype(jnp.bfloat16), 'shard', scatter_dimension=0,...  146 us
    reduce_scatter x2, waiting for transfers between devices, shards(): lax.psum_scatter(d_proj.astype(jnp.bfloat16), 'shard', scatter_dimension=...  136 us
    unnamed x251, local copies, waits for them, and re-layouts  92.5 us
    all_gather x2, waiting for transfers between devices, shards(): lax.all_gather(down_weight[layer_at], 'shard', axis=0, tiled=True)  88.2 us
    psum x1, waiting for transfers between devices, shards(): lax.psum(g_qkv.astype(jnp.bfloat16), 'rep').astype(jnp.float32)  77 us
    psum x1, waiting for transfers between devices, shards(): lax.psum(g_proj.astype(jnp.bfloat16), 'rep').astype(jnp.float32)  72.4 us
  transfers between devices with their start and end apart: 30, of which 27 were waited for; matrix products, arithmetic and copies ran while one was open for 9% of the time, Pallas kernels for 0%

commit v1 on v0

v1 whole, which is shorter than its diff:
```python
import functools

import jax
import jax.numpy as jnp
from jax import lax
from jax.experimental import pallas as pl
from jax.experimental.pallas import tpu as pltpu
from jax.sharding import PartitionSpec as P

MESH = pl.DeviceIdType.MESH
F32 = jnp.float32
BF16 = jnp.bfloat16
H, HD, D, FF, LAYERS = 8, 64, 512, 2048, 2
ZH, Y, CORES = 2, 4, 2
GROUP = ZH * Y * CORES
ROWS = 64
TOK = 2 * ROWS
LENGTH = GROUP * ROWS
QB = 256
NQ = LENGTH // QB
QKV, PROJ, UP, DOWN = range(4)
SHARD = ((32, 3 * D), (32, D), (32, FF), (128, D))


def nn(a, b):
    return jnp.dot(a, b, preferred_element_type=F32)


def nt(a, b):
    return lax.dot_general(a, b, (((1,), (1,)), ((), ())), preferred_element_type=F32)


def tn(a, b):
    return lax.dot_general(a, b, (((0,), (0,)), ((), ())), preferred_element_type=F32)


def norm_forward(values, gain, shift):
    center = values - jnp.mean(values, axis=-1, keepdims=True)
    spread = jnp.mean(center * center, axis=-1, keepdims=True)
    scale = lax.rsqrt(spread + 1e-06)
    unit = center * scale
    return unit * gain + shift, unit, scale


def norm_backward(grad, unit, scale, gain):
    d_unit = grad * gain
    first = jnp.mean(d_unit, axis=-1, keepdims=True)
    second = jnp.mean(d_unit * unit, axis=-1, keepdims=True)
    d_gain = jnp.sum(grad * unit, axis=0, keepdims=True)
    d_shift = jnp.sum(grad, axis=0, keepdims=True)
    return scale * (d_unit - first - unit * second), d_gain, d_shift


def column_sum(values):
    return jnp.sum(values, axis=0, keepdims=True)


def wait_bytes(ref, sem):
    pltpu.make_async_copy(ref, ref, sem).wait()


class Place:
    def __init__(self, nx, nzl):
        self.nx, self.nzl, self.nz = nx, nzl, ZH * nzl
        rep, shard = lax.axis_index("rep"), lax.axis_index("shard")
        self.rep, self.shard = rep, shard
        self.zl, self.x = lax.div(rep, nx), lax.rem(rep, nx)
        self.zh, self.y = lax.div(shard, Y * CORES), lax.rem(lax.div(shard, CORES), Y)
        self.core = lax.rem(shard, CORES)
        self.z = self.zh * nzl + self.zl

    def at(self, x=None, y=None, z=None, core=None):
        x = self.x if x is None else x
        y = self.y if y is None else y
        z = self.z if z is None else z
        core = self.core if core is None else core
        zh, zl = lax.div(z, self.nzl), lax.rem(z, self.nzl)
        return (zl * self.nx + x, zh * (Y * CORES) + y * CORES + core)

    def xs(self, d):
        return lax.rem(self.x + d, self.nx)

    def ys(self, d):
        return lax.rem(self.y + d, Y)

    def zs(self, d):
        return lax.rem(self.z + d, self.nz)

    def peers(self):
        found = []
        for dy in range(Y):
            for dz in range(self.nz):
                if dy or dz:
                    found.append(self.at(y=self.ys(dy), z=self.zs(dz)))
        for dx in range(1, self.nx):
            for dz in range(self.nz):
                found.append(self.at(x=self.xs(dx), z=self.zs(dz)))
        for dy in range(Y):
            for zh in range(ZH):
                z = lax.rem(self.z + zh * self.nzl, self.nz)
                found.append(self.at(y=self.ys(dy), z=z, core=1 - self.core))
        return found


def remote(src, dst, send_sem, recv_sem, device):
    pltpu.make_async_remote_copy(
        src_ref=src, dst_ref=dst, send_sem=send_sem, recv_sem=recv_sem, device_id=device, device_id_type=MESH
    ).start()


class Exchange:
    def __init__(self, place, out, into, sems):
        self.place, self.out, self.into, self.sems = place, out, into, sems

    def start(self):
        me = self.place.shard
        for d in range(1, GROUP):
            to = lax.rem(me + d, GROUP)
            remote(self.out.at[to], self.into.at[me], self.sems.at[0], self.sems.at[1], (self.place.rep, to))
        self.into[me] = self.out[me]

    def wait(self):
        wait_bytes(self.into.at[pl.ds(0, GROUP - 1)], self.sems.at[1])

    def finish(self):
        wait_bytes(self.out.at[pl.ds(0, GROUP - 1)], self.sems.at[0])


class Weight:
    def __init__(self, place, own, full, sems, sums, axis, result):
        self.place, self.own, self.full, self.sems = place, own, full, sems
        self.pair, self.chip, self.recv1, self.sum1, self.recv2, self.recv3 = sums
        self.axis, self.result = axis, result
        self.rows, self.cols = own.shape

    def sem(self, i):
        return self.sems.at[i]

    def g0(self):
        p, full = self.place, self.full
        slot = full.at[p.zh, p.y, p.core]
        slot[...] = self.own[...]
        for d in (1, 3, 2):
            remote(self.own, slot, self.sem(0), self.sem(4), p.at(y=p.ys(d)))
        remote(self.own, slot, self.sem(0), self.sem(3), p.at(z=p.nz - 1 - p.z))

    def g1(self):
        p, full = self.place, self.full
        slot = full.at[1 - p.zh, p.y, p.core]
        wait_bytes(full.at[0, 0, 0], self.sem(3))
        for d in (1, 3, 2):
            remote(slot, slot, self.sem(1), self.sem(5), p.at(y=p.ys(d)))

    def g2(self):
        p, full = self.place, self.full
        wait_bytes(full.at[0, pl.ds(0, 3), 0], self.sem(4))
        half = full.at[p.zh, :, p.core]
        remote(half, half, self.sem(2), self.sem(6), p.at(core=1 - p.core))

    def g3(self):
        p, full = self.place, self.full
        wait_bytes(full.at[0, pl.ds(0, 3), 0], self.sem(5))
        half = full.at[1 - p.zh, :, p.core]
        remote(half, half, self.sem(2), self.sem(6), p.at(core=1 - p.core))

    def g4(self):
        wait_bytes(self.full.at[:, :, 0], self.sem(6))

    def sent(self):
        full = self.full
        wait_bytes(full.at[0, :, 0], self.sem(0))
        wait_bytes(full.at[0, pl.ds(0, 3), 0], self.sem(1))
        wait_bytes(full.at[:, :, 0], self.sem(2))

    def value(self):
        return self.full[...].reshape(GROUP * self.rows, self.cols)

    def store(self, start, block):
        count = block.shape[0]
        per_y = CORES * self.rows
        block = block.astype(BF16)
        if count == Y * per_y:
            self.full[start // count] = block.reshape(Y, CORES, self.rows, self.cols)
        else:
            n = count // per_y
            zh, y = divmod(start // per_y, Y)
            self.full[zh, y : y + n] = block.reshape(n, CORES, self.rows, self.cols)

    def e0(self):
        p, full = self.place, self.full
        remote(full.at[:, :, 1 - p.core], self.pair, self.sem(7), self.sem(8), p.at(core=1 - p.core))

    def e1(self):
        p = self.place
        nx, nzl = p.nx, p.nzl
        half, part = self.rows // nzl, self.cols // nx
        wait_bytes(self.pair, self.sem(8))
        for zh in range(ZH):
            for y in range(Y):
                total = self.full[zh, y, p.core].astype(F32) + self.pair[zh, y].astype(F32)
                total = total.astype(BF16)
                for x in range(nx):
                    for zl in range(nzl):
                        a, b = (y, x) if self.axis == "y" else (x, y)
                        self.chip[a, b, zh * nzl + zl] = total[
                            zl * half : (zl + 1) * half, x * part : (x + 1) * part
                        ]
        na = Y if self.axis == "y" else nx
        for d in (1, 3, 2)[: na - 1] if na == 4 else range(1, na):
            if self.axis == "y":
                to, device = p.ys(d), p.at(y=p.ys(d))
            else:
                to, device = p.xs(d), p.at(x=p.xs(d))
            remote(self.chip.at[to], self.recv1.at[d - 1], self.sem(9), self.sem(10), device)

    def e2(self):
        p = self.place
        na, nb = (Y, p.nx) if self.axis == "y" else (p.nx, Y)
        a, b = (p.y, p.x) if self.axis == "y" else (p.x, p.y)
        if na > 1:
            wait_bytes(self.recv1, self.sem(10))
        for at in range(nb):
            for z in range(p.nz):
                total = self.chip[a, at, z].astype(F32)
                for d in range(na - 1):
                    total = total + self.recv1[d, at, z].astype(F32)
                self.sum1[at, z] = total.astype(BF16)
        for db in range(nb):
            for dz in range(p.nz):
                if db == 0 and dz == 0:
                    continue
                to_b, to_z = lax.rem(b + db, nb), p.zs(dz)
                device = p.at(x=to_b, z=to_z) if self.axis == "y" else p.at(y=to_b, z=to_z)
                remote(
                    self.sum1.at[to_b, to_z],
                    self.recv2.at[db * p.nz + dz - 1],
                    self.sem(11),
                    self.sem(12),
                    device,
                )

    def e3(self):
        p = self.place
        b = p.x if self.axis == "y" else p.y
        wait_bytes(self.recv2, self.sem(12))
        total = self.sum1[b, p.z].astype(F32)
        for i in range(self.recv2.shape[0]):
            total = total + self.recv2[i].astype(F32)
        slot = self.recv3.at[p.rep]
        slot[...] = total.astype(BF16)
        nrep = p.nx * p.nzl
        for d in range(1, nrep):
            remote(slot, slot, self.sem(13), self.sem(14), (lax.rem(p.rep + d, nrep), p.shard))

    def e4(self):
        p = self.place
        nx, nzl = p.nx, p.nzl
        half, part = self.rows // nzl, self.cols // nx
        if nx * nzl > 1:
            wait_bytes(self.recv3.at[pl.ds(0, nx * nzl - 1)], self.sem(14))
        for zl in range(nzl):
            for x in range(nx):
                self.result[zl * half : (zl + 1) * half, x * part : (x + 1) * part] = self.recv3[
                    zl * nx + x
                ].astype(F32)

    def reduced(self):
        p = self.place
        wait_bytes(self.pair, self.sem(7))
        if self.recv1.shape[0] and (Y if self.axis == "y" else p.nx) > 1:
            wait_bytes(self.recv1, self.sem(9))
        wait_bytes(self.recv2, self.sem(11))
        if p.nx * p.nzl > 1:
            wait_bytes(self.recv3.at[pl.ds(0, p.nx * p.nzl - 1)], self.sem(13))


def side_by_side(block):
    n = block.shape[-2] // 2
    return jnp.concatenate([block[..., :n, :], block[..., n:, :]], axis=-1)


def one_above_other(block):
    return jnp.concatenate([block[..., :HD], block[..., HD:]], axis=-2)


def split_heads(joined, slots):
    for s in range(2):
        rows = joined[s * ROWS : (s + 1) * ROWS]
        for h in range(H):
            at = h * HD
            query, key = rows[:, at : at + HD], rows[:, D + at : D + at + HD]
            slots[s * H + h, 0:ROWS] = jnp.concatenate([query, key], axis=1)
            slots[s * H + h, ROWS:96] = side_by_side(rows[:, 2 * D + at : 2 * D + at + HD])


def split_context(context, slots):
    for s in range(2):
        rows = context[s * ROWS : (s + 1) * ROWS]
        for h in range(H):
            slots[s * H + h] = side_by_side(rows[:, h * HD : (h + 1) * HD])


def join_context(slots):
    parts = []
    for s in range(2):
        heads = [one_above_other(slots[s * H + h]) for h in range(H)]
        parts.append(jnp.concatenate(heads, axis=1))
    return jnp.concatenate(parts, axis=0)


def join_heads(slots):
    parts = []
    for s in range(2):
        both = [slots[s * H + h] for h in range(H)]
        queries = [block[0:ROWS, :HD] for block in both]
        keys = [block[0:ROWS, HD:] for block in both]
        values = [one_above_other(block[ROWS:96]) for block in both]
        parts.append(jnp.concatenate(queries + keys + values, axis=1))
    return jnp.concatenate(parts, axis=0)


def head_parts(slots):
    both = slots[:, 0:ROWS, :].reshape(LENGTH, 2 * HD)
    values = one_above_other(slots[:, ROWS:96, :]).reshape(LENGTH, HD)
    queries = (both[:, :HD].astype(F32) * 0.125).astype(BF16)
    return queries, both[:, HD:], values


def kernel(nx, nzl, *refs):
    refs = list(refs)

    def take(n):
        got = refs[:n]
        del refs[:n]
        return got

    x_ref, cot_ref = take(2)
    own = take(4)
    bias_ref, gain_ref, shift_ref, upb_ref = take(4)
    out_ref, dx_ref = take(2)
    results = take(4)
    bias_out, gain_out, shift_out, upb_out = take(4)
    full = [take(4) for _ in range(LAYERS)]
    sums = [[take(6) for _ in range(4)] for _ in range(LAYERS)]
    swaps = [take(8) for _ in range(LAYERS)]
    small_own, small_all, small_grad, small_in, small_rep = take(5)
    small, small_up, d_small, d_small_up = take(4)
    saved = [take(8) for _ in range(LAYERS)]
    probs = take(LAYERS)
    query_ref, dc_ref, ctx_ref, dq_ref, dk_ref, dv_ref = take(6)
    weight_sems, swap_sems, small_sems = take(3)

    p = Place(nx, nzl)
    weights = [
        [
            Weight(
                p,
                own[w].at[l],
                full[l][w],
                weight_sems.at[l * 4 + w],
                sums[l][w],
                "y",
                results[w].at[l],
            )
            for w in range(4)
        ]
        for l in range(LAYERS)
    ]
    swap = [
        [Exchange(p, swaps[l][2 * i], swaps[l][2 * i + 1], swap_sems.at[l * 4 + i]) for i in range(4)]
        for l in range(LAYERS)
    ]

    barrier = pltpu.get_barrier_semaphore()
    peers = p.peers()
    for peer in peers:
        pl.semaphore_signal(barrier, inc=1, device_id=peer, device_id_type=MESH)
    small_own[...] = jnp.zeros_like(small_own)
    for l in range(LAYERS):
        at = l * 8
        small_own[at : at + 1, :] = upb_ref[l : l + 1, :].astype(F32)
        small_own[at + 1 : at + 4, 0:32] = bias_ref[l].astype(F32)
        small_own[at + 4 : at + 6, 0:32] = gain_ref[l].astype(F32)
        small_own[at + 6 : at + 8, 0:32] = shift_ref[l].astype(F32)
    pl.semaphore_wait(barrier, len(peers))

    me = p.shard
    order = [weights[l][w] for l in range(LAYERS) for w in range(4)]
    order[0].g0()
    for d in range(1, GROUP):
        to = lax.rem(me + d, GROUP)
        remote(small_own, small_all.at[me], small_sems.at[0], small_sems.at[1], (p.rep, to))
    small_all[me] = small_own[...]
    for weight in order[1:]:
        weight.g0()
    order[0].g1()
    order[0].g2()
    order[1].g1()
    order[2].g1()
    order[3].g1()

    wait_bytes(small_all.at[pl.ds(0, GROUP - 1)], small_sems.at[1])
    for l in range(LAYERS):
        for q in range(4):
            part = [small_all[4 * q + i, l * 8 : l * 8 + 8, 0:32] for i in range(4)]
            small[l, :, q * 128 : (q + 1) * 128] = jnp.concatenate(part, axis=1)
        for t in range(GROUP):
            small_up[l, :, t * 128 : (t + 1) * 128] = small_all[t, l * 8 : l * 8 + 1, :]

    order[0].g3()

    hidden = x_ref[...].astype(F32)
    for l in range(LAYERS):
        qkv, proj, up, down = weights[l]
        to_heads, to_tokens, _, _ = swap[l]
        source_ref, unit1, scale1, unit2, scale2, mid_ref, act_ref, slope_ref = saved[l]
        source = hidden.astype(BF16)
        source_ref[...] = source
        qkv.g4()
        joined = nn(source, qkv.value())
        value_bias = small[l, 1:2, :]
        joined = jnp.concatenate([joined[:, : 2 * D], joined[:, 2 * D :] + value_bias], axis=1)
        split_heads(joined.astype(BF16), to_heads.out)
        to_heads.start()
        proj.g2()
        proj.g3()
        if l + 1 < LAYERS:
            for weight in weights[l + 1]:
                weight.g1()
        to_heads.wait()
        queries, keys, values = head_parts(to_heads.into[...])
        query_ref[...] = queries.reshape(NQ, QB, HD)
        values_t = values.T

        def attend(i, carry):
            scores = nt(keys, query_ref[i])
            expo = jnp.exp(scores - jnp.max(scores, axis=0, keepdims=True))
            prob = expo * (1.0 / jnp.sum(expo, axis=0, keepdims=True))
            probs[l][i] = prob
            ctx_ref[i] = nn(values_t, prob.astype(BF16)).T.astype(BF16)
            return carry

        lax.fori_loop(0, NQ, attend, 0)
        context = ctx_ref[...].reshape(GROUP, ROWS, HD)
        to_tokens.out[...] = side_by_side(context)
        to_tokens.start()
        up.g2()
        up.g3()
        proj.g4()
        to_tokens.wait()
        context = join_context(to_tokens.into)
        first = hidden + nn(context, proj.value()) + small[l, 2:3, :]
        middle, unit, scale = norm_forward(first, small[l, 4:5, :], small[l, 6:7, :])
        unit1[...], scale1[...] = unit, scale
        mid_low = middle.astype(BF16)
        mid_ref[...] = mid_low
        up.g4()
        for j in range(4):
            at = j * 512
            upper = nn(mid_low, up.full[:, :, :, :, at : at + 512].reshape(D, 512))
            upper = upper + small_up[l, :, at : at + 512]
            phi = 0.5 + 0.5 * lax.erf(upper * (0.5**0.5))
            act_ref[:, at : at + 512] = (upper * phi).astype(BF16)
            density = jnp.exp(-0.5 * upper * upper) * 0.3989422804014327
            slope_ref[:, at : at + 512] = phi + upper * density
        down.g2()
        down.g3()
        down.g4()
        if l + 1 < LAYERS:
            weights[l + 1][0].g2()
            weights[l + 1][0].g3()
        second = middle + nn(act_ref[...], down.value()) + small[l, 3:4, :]
        hidden, unit, scale = norm_forward(second, small[l, 5:6, :], small[l, 7:8, :])
        unit2[...], scale2[...] = unit, scale
    out_ref[...] = hidden.astype(BF16)

    grad = cot_ref[...].astype(F32)
    pending = []
    for l in reversed(range(LAYERS)):
        qkv, proj, up, down = weights[l]
        to_heads, to_tokens, d_to_heads, d_to_tokens = swap[l]
        source_ref, unit1, scale1, unit2, scale2, mid_ref, act_ref, slope_ref = saved[l]
        grad_two, d_small[l, 5:6, :], d_small[l, 7:8, :] = norm_backward(
            grad, unit2[...], scale2[...], small[l, 5:6, :]
        )
        low_two = grad_two.astype(BF16)
        d_small[l, 3:4, :] = column_sum(low_two.astype(F32))
        down.sent()
        d_uppers = []
        for j in range(4):
            at = j * 512
            d_act = nt(low_two, down.full[j // 2, (j % 2) * 2 : (j % 2) * 2 + 2].reshape(512, D))
            d_upper = (d_act * slope_ref[:, at : at + 512]).astype(BF16)
            d_small_up[l, :, at : at + 512] = column_sum(d_upper.astype(F32))
            d_uppers.append(d_upper)
        d_upper = jnp.concatenate(d_uppers, axis=1)
        for j in range(8):
            down.store(j * 256, tn(act_ref[:, j * 256 : (j + 1) * 256], low_two))
        down.e0()
        grad_mid = grad_two + nt(d_upper, up.value())
        up.sent()
        for j in range(2):
            up.store(j * 256, tn(mid_ref[:, j * 256 : (j + 1) * 256], d_upper))
        up.e0()
        grad_one, d_small[l, 4:5, :], d_small[l, 6:7, :] = norm_backward(
            grad_mid, unit1[...], scale1[...], small[l, 4:5, :]
        )
        low_one = grad_one.astype(BF16)
        d_small[l, 2:3, :] = column_sum(low_one.astype(F32))
        d_context = nt(low_one, proj.value()).astype(BF16)
        split_context(d_context, d_to_heads.out)
        d_to_heads.start()
        context = join_context(to_tokens.into)
        proj.sent()
        for j in range(2):
            proj.store(j * 256, tn(context[:, j * 256 : (j + 1) * 256], low_one))
        proj.e0()
        down.e1()
        for step in pending:
            step()
        pending = []
        d_to_heads.wait()
        queries, keys, values = head_parts(to_heads.into[...])
        query_ref[...] = queries.reshape(NQ, QB, HD)
        dc_ref[...] = one_above_other(d_to_heads.into[...]).reshape(NQ, QB, HD)
        keys_t = keys.T
        dk_ref[...] = jnp.zeros_like(dk_ref)
        dv_ref[...] = jnp.zeros_like(dv_ref)

        def attend_back(i, carry):
            d_ctx = dc_ref[i]
            d_prob = nt(values, d_ctx)
            prob = probs[l][i]
            row = jnp.sum(prob * d_prob, axis=0, keepdims=True)
            d_score = (prob * (d_prob - row)).astype(BF16)
            dv_ref[...] += nn(prob.astype(BF16), d_ctx)
            dk_ref[...] += nn(d_score, query_ref[i])
            dq_ref[i] = (nn(keys_t, d_score) * 0.125).T.astype(BF16)
            return carry

        lax.fori_loop(0, NQ, attend_back, 0)
        both = jnp.concatenate([dq_ref[...].reshape(LENGTH, HD), dk_ref[...].astype(BF16)], axis=1)
        d_to_tokens.out[:, 0:ROWS, :] = both.reshape(GROUP, ROWS, 2 * HD)
        d_to_tokens.out[:, ROWS:96, :] = side_by_side(dv_ref[...].astype(BF16).reshape(GROUP, ROWS, HD))
        d_to_tokens.start()
        up.e1()
        down.e2()
        d_to_tokens.wait()
        d_joined = join_heads(d_to_tokens.into)
        d_small[l, 1:2, :] = column_sum(d_joined[:, 2 * D :].astype(F32))
        grad = grad_one + nt(d_joined, qkv.value())
        qkv.sent()
        for j in range(2):
            qkv.store(j * 256, tn(source_ref[:, j * 256 : (j + 1) * 256], d_joined))
        qkv.e0()
        proj.e1()
        up.e2()
        down.e3()
        if l > 0:
            pending = [qkv.e1, proj.e2, up.e3, down.e4]
            rest = [qkv.e2, proj.e3, up.e4, qkv.e3, proj.e4, qkv.e4]
    dx_ref[...] = grad

    small_grad[...] = jnp.zeros_like(small_grad)
    for l in range(LAYERS):
        for t in range(GROUP):
            small_grad[t, l * 8 + 1 : l * 8 + 8, 0:32] = d_small[l, 1:8, t * 32 : (t + 1) * 32]
            small_grad[t, l * 8 : l * 8 + 1, :] = d_small_up[l, :, t * 128 : (t + 1) * 128]
    for d in range(1, GROUP):
        to = lax.rem(me + d, GROUP)
        remote(small_grad.at[to], small_in.at[me], small_sems.at[2], small_sems.at[3], (p.rep, to))
    small_in[me] = small_grad[me]

    qkv, proj, up, down = weights[0]
    for step in rest[:3]:
        step()
    qkv.e1()
    proj.e2()
    up.e3()
    wait_bytes(small_in.at[pl.ds(0, GROUP - 1)], small_sems.at[3])
    total = small_in[0]
    for t in range(1, GROUP):
        total = total + small_in[t]
    slot = small_rep.at[p.rep]
    slot[...] = total
    nrep = nx * nzl
    for d in range(1, nrep):
        remote(slot, slot, small_sems.at[4], small_sems.at[5], (lax.rem(p.rep + d, nrep), me))
    for step in rest[3:]:
        step()
    down.e4()
    qkv.e2()
    proj.e3()
    up.e4()
    qkv.e3()
    proj.e4()
    if nrep > 1:
        wait_bytes(small_rep.at[pl.ds(0, nrep - 1)], small_sems.at[5])
    total = small_rep[0]
    for t in range(1, nrep):
        total = total + small_rep[t]
    for l in range(LAYERS):
        at = l * 8
        upb_out[l : l + 1, :] = total[at : at + 1, :]
        bias_out[l] = total[at + 1 : at + 4, 0:32]
        gain_out[l] = total[at + 4 : at + 6, 0:32]
        shift_out[l] = total[at + 6 : at + 8, 0:32]
    qkv.e4()

    for weight in order:
        weight.reduced()
    for l in range(LAYERS):
        for one in swap[l]:
            one.finish()
    wait_bytes(small_all.at[pl.ds(0, GROUP - 1)], small_sems.at[0])
    wait_bytes(small_grad.at[pl.ds(0, GROUP - 1)], small_sems.at[2])
    if nrep > 1:
        wait_bytes(small_rep.at[pl.ds(0, nrep - 1)], small_sems.at[4])


def scratch(nx, nzl):
    nz, nrep = ZH * nzl, nx * nzl
    shapes = []
    for _ in range(LAYERS):
        for r, c in SHARD:
            shapes.append(pltpu.VMEM((ZH, Y, CORES, r, c), BF16))
    for _ in range(LAYERS):
        for r, c in SHARD:
            piece = (r // nzl, c // nx)
            shapes.append(pltpu.VMEM((ZH, Y, r, c), BF16))
            shapes.append(pltpu.VMEM((Y, nx, nz) + piece, BF16))
            shapes.append(pltpu.VMEM((Y - 1, nx, nz) + piece, BF16))
            shapes.append(pltpu.VMEM((nx, nz) + piece, BF16))
            shapes.append(pltpu.VMEM((nx * nz - 1,) + piece, BF16))
            shapes.append(pltpu.VMEM((nrep,) + piece, BF16))
    for _ in range(LAYERS):
        for rows in (96, 32, 32, 96):
            shapes += [pltpu.VMEM((GROUP, rows, 128), BF16)] * 2
    shapes += [pltpu.VMEM((16, 128), F32)]
    shapes += [pltpu.VMEM((GROUP, 16, 128), F32)] * 3
    shapes += [pltpu.VMEM((nrep, 16, 128), F32)]
    shapes += [pltpu.VMEM((LAYERS, 8, D), F32), pltpu.VMEM((LAYERS, 1, FF), F32)] * 2
    for _ in range(LAYERS):
        shapes += [
            pltpu.VMEM((TOK, D), BF16),
            pltpu.VMEM((TOK, D), F32),
            pltpu.VMEM((TOK, 1), F32),
            pltpu.VMEM((TOK, D), F32),
            pltpu.VMEM((TOK, 1), F32),
            pltpu.VMEM((TOK, D), BF16),
            pltpu.VMEM((TOK, FF), BF16),
            pltpu.VMEM((TOK, FF), F32),
        ]
    shapes += [pltpu.VMEM((NQ, LENGTH, QB), F32)] * LAYERS
    shapes += [pltpu.VMEM((NQ, QB, HD), BF16)] * 4
    shapes += [pltpu.VMEM((LENGTH, HD), F32)] * 2
    shapes += [
        pltpu.SemaphoreType.DMA((LAYERS * 4, 15)),
        pltpu.SemaphoreType.DMA((LAYERS * 4, 2)),
        pltpu.SemaphoreType.DMA((6,)),
    ]
    return shapes


def solution(mesh):
    nrep = mesh.shape["rep"]
    nzl = 2 if nrep >= 2 else 1
    nx = nrep // nzl

    def shards(inputs, *arguments):
        cotangent, members = arguments[-1], arguments[:-1]
        shapes = [jax.ShapeDtypeStruct((TOK, D), BF16), jax.ShapeDtypeStruct((TOK, D), F32)]
        shapes += [jax.ShapeDtypeStruct(member.shape, F32) for member in members]
        got = pl.pallas_call(
            functools.partial(kernel, nx, nzl),
            out_shape=shapes,
            in_specs=[pl.BlockSpec(memory_space=pltpu.VMEM)] * 10,
            out_specs=[pl.BlockSpec(memory_space=pltpu.VMEM)] * 10,
            scratch_shapes=scratch(nx, nzl),
            compiler_params=pltpu.CompilerParams(
                collective_id=0, has_side_effects=True, vmem_limit_bytes=63 * 1024 * 1024
            ),
            cost_estimate=pl.CostEstimate(flops=7 * 10**9, bytes_accessed=8 * 10**6, transcendentals=5 * 10**6),
        )(inputs.reshape(TOK, D), cotangent.reshape(TOK, D), *members)
        return (got[0].reshape(inputs.shape), got[1].reshape(inputs.shape), *got[2:])

    rows, columns = P(None, "shard", None), P(None, None, "shard")
    both = P("rep", "shard", None)
    weights = (rows, rows, rows, rows, columns, columns, columns, P(None, "shard"))
    return jax.shard_map(
        shards,
        mesh=mesh,
        in_specs=(both, *weights, both),
        out_specs=(both, both, *weights),
        check_vma=False,
    )
```

time: 2080 us -> 233 us (0.11)
  waiting for transfers between devices: 1520 us -> 0 us
  blocking collectives: 250 us -> 0 us
  Pallas kernels: 0 us -> 221 us
  local copies, waits for them, and re-layouts: 165 us -> 10.5 us
  matrix products: 87 us -> 0 us
  other arithmetic: 28.4 us -> 0 us
    unnamed x42 -> x0, waiting for transfers between devices: 715 us -> none
    reduce_scatter x6 -> x0, waiting for transfers between devices: 429 us -> none  [the longest x2 148 us: shards(): lax.psum_scatter(d_down.astype(jnp.bfloat16), 'shard', scatter_dimension=...]
    all_gather x10 -> x0, waiting for transfers between devices: 223 us -> none  [the longest x2 88.2 us: shards(): lax.all_gather(down_weight[layer_at], 'shard', axis=0, tiled=True)]
    pallas_call x0 -> x1, Pallas kernels: none -> 221 us  [shards(): pl.pallas_call(functools.partial(kernel, nx, nzl), out_shape=shapes, in_s...]
    all_gather x10 -> x0, blocking collectives: 216 us -> none  [the longest x2 46.8 us: shards(): lax.all_gather(bias_rows[layer_at], 'shard', axis=1, tiled=True)]
    psum x2 -> x0, waiting for transfers between devices: 149 us -> none  [the longest x1 77 us: shards(): lax.psum(g_qkv.astype(jnp.bfloat16), 'rep').astype(jnp.float32)]
    dot_general x36 -> x0, matrix products: 87 us -> none  [the longest x8 15.2 us: left_product(): lax.dot_general(first_op, second_op, (((0,), (0,)), ((), ())), preferred_...]
    unnamed x251 -> x29, local copies, waits for them, and re-layouts: 92.5 us -> 10.5 us
  transfers between devices with their start and end apart: 30 -> 0, of which waited for: 27 -> 0; matrix products, arithmetic and copies ran while one was open for 9% -> 0% of each run, Pallas kernels for 0% -> 0%
where the time goes in v1:
time: 233 us; the launch traced here: 232 us
  Pallas kernels  221 us (95%)
  local copies, waits for them, and re-layouts  10.5 us (5%)
    pallas_call x1, Pallas kernels, shards(): pl.pallas_call(functools.partial(kernel, nx, nzl), out_shape=shapes, in_s...  221 us
    unnamed x29, local copies, waits for them, and re-layouts  10.5 us

profile of v1, /device:TPU:0, one launch (start us, length us, event | category | flops | bytes accessed | tf_op | source)
XLA Modules:
  0.0 232.2 jit_solution(7875070980553643250)
XLA Ops:
  0.6 0.0 copy-start.7
  0.7 0.7 copy-done.7
  1.3 0.6 copy.20.refs_6_
  1.9 221.1 %shard_map.177 = (bf16[128,512]{1,0:T(8,128)(2,1)}, f32[128,512]{1,0:T(8,128)}, f32[2,32,1536]{2,1,0:T(8,128)}, f32[2,32,512]{2,1,0:T(8,128)}, f32[2,32,2048]{2,...) custom-call(bf16[128,512]{1,0:T(8,128)(2,1)} %bitcast.6, ...), custom_call_target="tpu_custom_call" | custom-call | flops 7000000000 | bytes 8000000 | tf_op jit(solution)/shard_map/pallas_call | solution.py:674
  223.0 0.0 copy-start.3
  223.0 1.3 copy.21
  224.3 0.0 copy-start.2
  224.3 1.6 copy.31
  225.9 0.0 copy-done.3
  225.9 0.7 copy.32
  226.6 0.0 copy-done.2
  226.6 0.0 copy-start.4
  226.7 0.0 copy-start.1
  226.7 0.7 copy.33
  227.4 0.2 copy-done.4
  227.6 0.7 copy.34
  228.3 0.0 copy-done.1
  228.3 0.0 copy-start
  228.3 0.8 copy.35
  229.1 0.4 copy-done
  229.5 0.0 copy-start.6
  229.5 0.8 copy.36
  230.3 0.0 copy-done.6
  230.3 0.0 copy-start.5
  230.3 0.6 copy.37
  230.9 0.1 copy-done.5
  231.0 0.0 copy-start.8
  231.0 0.6 copy.38
  231.6 0.1 copy-done.8
  231.7 0.6 copy.39
Async XLA Ops:
  0.6 0.7 copy-start.7
  223.0 2.9 %copy-start.3 = (f32[128,512]{1,0:T(8,128)S(1)}, f32[128,512]{1,0:T(8,128)}, u32[]{:S(2)}) copy-start(f32[128,512]{1,0:T(8,128)} %get-tuple-element.21) | copy-start | bytes 786436
  224.3 2.3 %copy-start.2 = (f32[2,32,1536]{2,1,0:T(8,128)S(1)}, f32[2,32,1536]{2,1,0:T(8,128)}, u32[]{:S(2)}) copy-start(f32[2,32,1536]{2,1,0:T(8,128)} %get-tuple-element.52) | copy-start | bytes 1179652
  226.6 1.0 copy-start.4
  226.7 1.7 copy-start.1
  228.3 1.2 copy-start
  229.5 0.8 copy-start.6
  230.3 0.7 copy-start.5
  231.0 0.7 copy-start.8

commit v2 on v1

v2 whole, which is shorter than its diff:
```python
import functools

import jax
import jax.numpy as jnp
from jax import lax
from jax.experimental import pallas as pl
from jax.experimental.pallas import tpu as pltpu
from jax.sharding import PartitionSpec as P

MESH = pl.DeviceIdType.MESH
F32 = jnp.float32
BF16 = jnp.bfloat16
H, HD, D, FF, LAYERS = 8, 64, 512, 2048, 2
ZH, Y, CORES = 2, 4, 2
GROUP = ZH * Y * CORES
ROWS = 64
TOK = 2 * ROWS
LENGTH = GROUP * ROWS
QB = 256
NQ = LENGTH // QB
QKV, PROJ, UP, DOWN = range(4)
PARTS = (
    (QKV, 0, 32, 512, "x", "x"),
    (QKV, 512, 32, 512, "z", "y"),
    (QKV, 1024, 32, 512, "y", "x"),
    (PROJ, 0, 32, 512, "x", "y"),
    (UP, 0, 32, 1024, "x", "x"),
    (UP, 1024, 32, 1024, "z", "y"),
    (DOWN, 0, 128, 256, "x", "x"),
    (DOWN, 256, 128, 256, "y", "y"),
)
SEMS = 17


def nn(a, b):
    return jnp.dot(a, b, preferred_element_type=F32)


def nt(a, b):
    return lax.dot_general(a, b, (((1,), (1,)), ((), ())), preferred_element_type=F32)


def tn(a, b):
    return lax.dot_general(a, b, (((0,), (0,)), ((), ())), preferred_element_type=F32)


def norm_forward(values, gain, shift):
    center = values - jnp.mean(values, axis=-1, keepdims=True)
    spread = jnp.mean(center * center, axis=-1, keepdims=True)
    scale = lax.rsqrt(spread + 1e-06)
    unit = center * scale
    return unit * gain + shift, unit, scale


def norm_backward(grad, unit, scale, gain):
    d_unit = grad * gain
    first = jnp.mean(d_unit, axis=-1, keepdims=True)
    second = jnp.mean(d_unit * unit, axis=-1, keepdims=True)
    d_gain = jnp.sum(grad * unit, axis=0, keepdims=True)
    d_shift = jnp.sum(grad, axis=0, keepdims=True)
    return scale * (d_unit - first - unit * second), d_gain, d_shift


def column_sum(values):
    return jnp.sum(values, axis=0, keepdims=True)


def wait_bytes(ref, sem):
    pltpu.make_async_copy(ref, ref, sem).wait()


class Place:
    def __init__(self, nx, nzl):
        self.nx, self.nzl, self.nz = nx, nzl, ZH * nzl
        rep, shard = lax.axis_index("rep"), lax.axis_index("shard")
        self.rep, self.shard = rep, shard
        self.zl, self.x = lax.div(rep, nx), lax.rem(rep, nx)
        self.zh, self.y = lax.div(shard, Y * CORES), lax.rem(lax.div(shard, CORES), Y)
        self.core = lax.rem(shard, CORES)
        self.z = self.zh * nzl + self.zl

    def at(self, x=None, y=None, z=None, core=None):
        x = self.x if x is None else x
        y = self.y if y is None else y
        z = self.z if z is None else z
        core = self.core if core is None else core
        zh, zl = lax.div(z, self.nzl), lax.rem(z, self.nzl)
        return (zl * self.nx + x, zh * (Y * CORES) + y * CORES + core)

    def xs(self, d):
        return lax.rem(self.x + d, self.nx)

    def ys(self, d):
        return lax.rem(self.y + d, Y)

    def zs(self, d):
        return lax.rem(self.z + d, self.nz)

    def group(self):
        steps = [(dy, dz, dc) for dy in (2, 1, 3, 0) for dz in (1, 0) for dc in range(CORES) if dy or dz or dc]
        steps.sort(key=lambda step: -(2 * min(step[0], 1) + 2 * step[1] + step[2]))
        found = []
        for dy, dz, dc in steps:
            z = lax.rem(self.z + dz * self.nzl, self.nz)
            found.append(self.at(y=self.ys(dy), z=z, core=lax.rem(self.core + dc, CORES))[1])
        return found

    def peers(self):
        found = []
        for dy in range(Y):
            for dz in range(self.nz):
                if dy or dz:
                    found.append(self.at(y=self.ys(dy), z=self.zs(dz)))
        for dx in range(1, self.nx):
            for dz in range(self.nz):
                found.append(self.at(x=self.xs(dx), z=self.zs(dz)))
        for dy in range(Y):
            for zh in range(ZH):
                z = lax.rem(self.z + zh * self.nzl, self.nz)
                found.append(self.at(y=self.ys(dy), z=z, core=1 - self.core))
        return found


def remote(src, dst, send_sem, recv_sem, device):
    pltpu.make_async_remote_copy(
        src_ref=src, dst_ref=dst, send_sem=send_sem, recv_sem=recv_sem, device_id=device, device_id_type=MESH
    ).start()


class Exchange:
    def __init__(self, place, out, into, sems):
        self.place, self.out, self.into, self.sems = place, out, into, sems

    def start(self):
        me = self.place.shard
        for to in self.place.group():
            remote(self.out.at[to], self.into.at[me], self.sems.at[0], self.sems.at[1], (self.place.rep, to))
        self.into[me] = self.out[me]

    def wait(self):
        wait_bytes(self.into.at[pl.ds(0, GROUP - 1)], self.sems.at[1])

    def finish(self):
        wait_bytes(self.out.at[pl.ds(0, GROUP - 1)], self.sems.at[0])


class Part:
    def __init__(self, place, own, full, sems, sums, far, near, result, out):
        self.place, self.own, self.full, self.sems = place, own, full, sems
        self.pair, self.chip, self.recv1, self.sum1, self.recv2, self.recv3 = sums
        self.far, self.near, self.result, self.out = far, near, result, out
        self.rows, self.cols = own.shape
        p = place
        self.n = {"x": p.nx, "y": Y, "z": p.nz}
        self.me = {"x": p.x, "y": p.y, "z": p.z}
        self.axes = {"x": "xyz", "y": "yxz", "z": "zxy"}[near]

    def sem(self, i):
        return self.sems.at[i]

    def sibling(self):
        return self.place.at(core=1 - self.place.core)

    def across(self):
        return self.place.nz - 1 - self.place.z

    def keep(self):
        p = self.place
        self.full[p.zh, p.y, p.core] = self.own[...]

    def quarter(self, ref, x):
        nx = self.place.nx
        if self.rows == 128:
            n = self.rows // nx
            return ref.at[..., pl.ds(pl.multiple_of(x * n, n), n), :]
        n = self.cols // nx
        return ref.at[..., pl.ds(pl.multiple_of(x * n, n), n)]

    def g0(self):
        p = self.place
        slot = self.full.at[p.zh, p.y, p.core]
        if self.far == "x":
            src, dst = self.quarter(self.own, p.x), self.quarter(slot, p.x)
            for d in (2, 1, 3, 0):
                remote(src, dst, self.sem(4), self.sem(1), p.at(y=p.ys(d), z=self.across()))
            for d in (2, 1, 3):
                remote(src, dst, self.sem(3), self.sem(0), p.at(y=p.ys(d)))
        else:
            if self.far == "y":
                remote(self.own, slot, self.sem(3), self.sem(0), p.at(z=self.across()))
            for d in (2, 1, 3):
                remote(self.own, slot, self.sem(4), self.sem(1), p.at(y=p.ys(d)))

    def g1(self):
        p, full = self.place, self.full
        if self.far == "x":
            wait_bytes(self.quarter(full.at[0, pl.ds(0, 3), 0], 0), self.sem(0))
            wait_bytes(self.quarter(full.at[0, :, 0], 0), self.sem(1))
            mine = self.quarter(full.at[:, :, p.core], p.x)
            for d in order_of(p.nx):
                remote(mine, mine, self.sem(5), self.sem(2), p.at(x=p.xs(d)))
        elif self.far == "y":
            wait_bytes(full.at[0, 0, 0], self.sem(0))
            slot = full.at[1 - p.zh, p.y, p.core]
            for d in (2, 1, 3):
                remote(slot, slot, self.sem(5), self.sem(2), p.at(y=p.ys(d)))
        else:
            wait_bytes(full.at[0, pl.ds(0, 3), 0], self.sem(1))
            half = full.at[p.zh, :, p.core]
            remote(half, half, self.sem(5), self.sem(2), p.at(z=self.across()))

    def g2(self):
        p, full = self.place, self.full
        if self.far == "x":
            if p.nx > 1:
                wait_bytes(full.at[:, pl.ds(0, p.nx - 1), 0], self.sem(2))
        elif self.far == "y":
            wait_bytes(full.at[0, pl.ds(0, 3), 0], self.sem(1))
            wait_bytes(full.at[0, pl.ds(0, 3), 0], self.sem(2))
        else:
            wait_bytes(full.at[0, :, 0], self.sem(2))
        both = full.at[:, :, p.core]
        remote(both, both, self.sem(6), self.sem(7), self.sibling())

    def g3(self):
        wait_bytes(self.full.at[:, :, 0], self.sem(7))

    def sent(self):
        full, nx = self.full, self.place.nx
        if self.far == "x":
            wait_bytes(self.quarter(full.at[0, pl.ds(0, 3), 0], 0), self.sem(3))
            wait_bytes(self.quarter(full.at[0, :, 0], 0), self.sem(4))
            if nx > 1:
                wait_bytes(full.at[:, pl.ds(0, nx - 1), 0], self.sem(5))
        elif self.far == "y":
            wait_bytes(full.at[0, 0, 0], self.sem(3))
            wait_bytes(full.at[0, pl.ds(0, 3), 0], self.sem(4))
            wait_bytes(full.at[0, pl.ds(0, 3), 0], self.sem(5))
        else:
            wait_bytes(full.at[0, pl.ds(0, 3), 0], self.sem(4))
            wait_bytes(full.at[0, :, 0], self.sem(5))
        wait_bytes(full.at[:, :, 0], self.sem(6))

    def value(self):
        return self.full[...].reshape(GROUP * self.rows, self.cols)

    def store(self, start, block):
        count = block.shape[0]
        per_y = CORES * self.rows
        block = block.astype(BF16)
        if count == ZH * Y * per_y:
            self.full[...] = block.reshape(ZH, Y, CORES, self.rows, self.cols)
        elif count == Y * per_y:
            self.full[start // count] = block.reshape(Y, CORES, self.rows, self.cols)
        else:
            n = count // per_y
            zh, y = divmod(start // per_y, Y)
            self.full[zh, y : y + n] = block.reshape(n, CORES, self.rows, self.cols)

    def piece(self, zl, x):
        p = self.place
        if self.rows == 128:
            n = self.rows // (p.nx * p.nzl)
            at = (zl * p.nx + x) * n
            return slice(at, at + n), slice(None)
        half, part = self.rows // p.nzl, self.cols // p.nx
        return slice(zl * half, (zl + 1) * half), slice(x * part, (x + 1) * part)

    def e0(self):
        p, full = self.place, self.full
        remote(full.at[:, :, 1 - p.core], self.pair, self.sem(8), self.sem(9), self.sibling())

    def e1(self):
        p = self.place
        wait_bytes(self.pair, self.sem(9))
        for zh in range(ZH):
            for y in range(Y):
                total = self.full[zh, y, p.core].astype(F32) + self.pair[zh, y].astype(F32)
                total = total.astype(BF16)
                for x in range(p.nx):
                    for zl in range(p.nzl):
                        at = {"x": x, "y": y, "z": zh * p.nzl + zl}
                        rows, cols = self.piece(zl, x)
                        self.chip[tuple(at[axis] for axis in self.axes)] = total[rows, cols]
        a = self.axes[0]
        for d in order_of(self.n[a]):
            to = lax.rem(self.me[a] + d, self.n[a])
            remote(self.chip.at[to], self.recv1.at[d - 1], self.sem(10), self.sem(11), p.at(**{a: to}))

    def e2(self):
        p = self.place
        a, b, c = self.axes
        nb, nc = self.n[b], self.n[c]
        if self.n[a] > 1:
            wait_bytes(self.recv1, self.sem(11))
        for ib in range(nb):
            total = self.chip[self.me[a], ib].astype(F32)
            for d in range(self.n[a] - 1):
                total = total + self.recv1[d, ib].astype(F32)
            self.sum1[ib] = total.astype(BF16)
        pairs = [(db, dc) for db in range(nb) for dc in range(nc) if db or dc]
        for db, dc in sorted(pairs, key=lambda at: -(min(at[0], 1) + min(at[1], 1))):
            to_b, to_c = lax.rem(self.me[b] + db, nb), lax.rem(self.me[c] + dc, nc)
            remote(
                self.sum1.at[to_b, to_c],
                self.recv2.at[db * nc + dc - 1],
                self.sem(12),
                self.sem(13),
                p.at(**{b: to_b, c: to_c}),
            )

    def e3(self):
        p = self.place
        _, b, c = self.axes
        wait_bytes(self.recv2, self.sem(13))
        total = self.sum1[self.me[b], self.me[c]].astype(F32)
        for i in range(self.recv2.shape[0]):
            total = total + self.recv2[i].astype(F32)
        slot = self.recv3.at[p.rep]
        slot[...] = total.astype(BF16)
        nrep = p.nx * p.nzl
        for d in range(1, nrep):
            remote(slot, slot, self.sem(14), self.sem(15), (lax.rem(p.rep + d, nrep), p.shard))

    def e4(self):
        p = self.place
        nrep = p.nx * p.nzl
        if nrep > 1:
            wait_bytes(self.recv3.at[pl.ds(0, nrep - 1)], self.sem(15))
        for zl in range(p.nzl):
            for x in range(p.nx):
                rows, cols = self.piece(zl, x)
                self.result[rows, cols] = self.recv3[zl * p.nx + x].astype(F32)
        pltpu.make_async_copy(self.result, self.out, self.sem(16)).start()

    def reduced(self):
        p = self.place
        wait_bytes(self.pair, self.sem(8))
        if self.n[self.axes[0]] > 1:
            wait_bytes(self.recv1, self.sem(10))
        wait_bytes(self.recv2, self.sem(12))
        if p.nx * p.nzl > 1:
            wait_bytes(self.recv3.at[pl.ds(0, p.nx * p.nzl - 1)], self.sem(14))
        pltpu.make_async_copy(self.result, self.out, self.sem(16)).wait()


def order_of(n):
    return (2, 1, 3) if n == 4 else tuple(range(1, n))


def side_by_side(block):
    n = block.shape[-2] // 2
    return jnp.concatenate([block[..., :n, :], block[..., n:, :]], axis=-1)


def one_above_other(block):
    return jnp.concatenate([block[..., :HD], block[..., HD:]], axis=-2)


def split_heads(joined, slots):
    for s in range(2):
        rows = joined[s * ROWS : (s + 1) * ROWS]
        for h in range(H):
            at = h * HD
            query, key = rows[:, at : at + HD], rows[:, D + at : D + at + HD]
            slots[s * H + h, 0:ROWS] = jnp.concatenate([query, key], axis=1)
            slots[s * H + h, ROWS:96] = side_by_side(rows[:, 2 * D + at : 2 * D + at + HD])


def split_context(context, slots):
    for s in range(2):
        rows = context[s * ROWS : (s + 1) * ROWS]
        for h in range(H):
            slots[s * H + h] = side_by_side(rows[:, h * HD : (h + 1) * HD])


def join_context(slots):
    parts = []
    for s in range(2):
        heads = [one_above_other(slots[s * H + h]) for h in range(H)]
        parts.append(jnp.concatenate(heads, axis=1))
    return jnp.concatenate(parts, axis=0)


def join_heads(slots):
    parts = []
    for s in range(2):
        both = [slots[s * H + h] for h in range(H)]
        queries = [block[0:ROWS, :HD] for block in both]
        keys = [block[0:ROWS, HD:] for block in both]
        values = [one_above_other(block[ROWS:96]) for block in both]
        parts.append(jnp.concatenate(queries + keys + values, axis=1))
    return jnp.concatenate(parts, axis=0)


def head_parts(slots):
    both = slots[:, 0:ROWS, :].reshape(LENGTH, 2 * HD)
    values = one_above_other(slots[:, ROWS:96, :]).reshape(LENGTH, HD)
    queries = (both[:, :HD].astype(F32) * 0.125).astype(BF16)
    return queries, both[:, HD:], values


def kernel(nx, nzl, *refs):
    refs = list(refs)

    def take(n):
        got = refs[:n]
        del refs[:n]
        return got

    x_ref, cot_ref = take(2)
    own = take(4)
    bias_ref, gain_ref, shift_ref, upb_ref = take(4)
    out_hbm, dx_hbm = take(2)
    result_hbm = take(4)
    bias_out, gain_out, shift_out, upb_out = take(4)
    out_ref, dx_ref = take(2)
    results = take(4)
    full = [take(len(PARTS)) for _ in range(LAYERS)]
    sums = [[take(6) for _ in PARTS] for _ in range(LAYERS)]
    swaps = [take(8) for _ in range(LAYERS)]
    small_own, small_all, small_grad, small_in, small_rep = take(5)
    small, small_up, d_small, d_small_up = take(4)
    saved = [take(8) for _ in range(LAYERS)]
    probs = take(LAYERS)
    query_ref, dc_ref, ctx_ref, dq_ref, dk_ref, dv_ref = take(6)
    part_sems, swap_sems, small_sems, out_sems = take(4)

    p = Place(nx, nzl)
    parts = []
    for l in range(LAYERS):
        row = []
        for i, (w, at, _, cols, far, near) in enumerate(PARTS):
            here = pl.ds(at, cols)
            row.append(
                Part(
                    p,
                    own[w].at[l, :, here],
                    full[l][i],
                    part_sems.at[l * len(PARTS) + i],
                    sums[l][i],
                    far,
                    near,
                    results[w].at[l, :, here],
                    result_hbm[w].at[l, :, here],
                )
            )
        parts.append(row)
    swap = [
        [Exchange(p, swaps[l][2 * i], swaps[l][2 * i + 1], swap_sems.at[l * 4 + i]) for i in range(4)]
        for l in range(LAYERS)
    ]
    everything = [part for row in parts for part in row]

    for part in everything:
        part.keep()
    small_own[...] = jnp.zeros_like(small_own)
    for l in range(LAYERS):
        at = l * 8
        small_own[at : at + 1, :] = upb_ref[l : l + 1, :].astype(F32)
        small_own[at + 1 : at + 4, 0:32] = bias_ref[l].astype(F32)
        small_own[at + 4 : at + 6, 0:32] = gain_ref[l].astype(F32)
        small_own[at + 6 : at + 8, 0:32] = shift_ref[l].astype(F32)
    small_all[p.shard] = small_own[...]
    barrier = pltpu.get_barrier_semaphore()
    peers = p.peers()
    for peer in peers:
        pl.semaphore_signal(barrier, inc=1, device_id=peer, device_id_type=MESH)
    pl.semaphore_wait(barrier, len(peers))

    me = p.shard

    def run(which, *steps):
        for step in steps:
            for part in which:
                getattr(part, step)()

    early, late = parts[0][:3], parts[0][3:]
    run(early, "g0")
    for to in p.group():
        remote(small_own, small_all.at[me], small_sems.at[0], small_sems.at[1], (p.rep, to))
    run(late, "g0")
    run(early, "g1")
    run(late, "g1")
    wait_bytes(small_all.at[pl.ds(0, GROUP - 1)], small_sems.at[1])
    for l in range(LAYERS):
        for q in range(4):
            part = [small_all[4 * q + i, l * 8 : l * 8 + 8, 0:32] for i in range(4)]
            small[l, :, q * 128 : (q + 1) * 128] = jnp.concatenate(part, axis=1)
        for t in range(GROUP):
            small_up[l, :, t * 128 : (t + 1) * 128] = small_all[t, l * 8 : l * 8 + 1, :]
    run(early, "g2", "g3")

    hidden = x_ref[...].astype(F32)
    for l in range(LAYERS):
        proj, up, down = parts[l][3], parts[l][4:6], parts[l][6:8]
        to_heads, to_tokens, _, _ = swap[l]
        source_ref, unit1, scale1, unit2, scale2, mid_ref, act_ref, slope_ref = saved[l]
        source = hidden.astype(BF16)
        source_ref[...] = source
        joined = [nn(source, part.value()) for part in parts[l][:3]]
        joined[2] = joined[2] + small[l, 1:2, :]
        split_heads(jnp.concatenate(joined, axis=1).astype(BF16), to_heads.out)
        to_heads.start()
        if l + 1 < LAYERS:
            run(parts[l + 1], "g0")
        run([proj], "g2")
        to_heads.wait()
        queries, keys, values = head_parts(to_heads.into[...])
        query_ref[...] = queries.reshape(NQ, QB, HD)
        values_t = values.T

        def attend(i, carry):
            scores = nt(keys, query_ref[i])
            expo = jnp.exp(scores - jnp.max(scores, axis=0, keepdims=True))
            prob = expo * (1.0 / jnp.sum(expo, axis=0, keepdims=True))
            probs[l][i] = prob
            ctx_ref[i] = nn(values_t, prob.astype(BF16)).T.astype(BF16)
            return carry

        lax.fori_loop(0, NQ, attend, 0)
        context = ctx_ref[...].reshape(GROUP, ROWS, HD)
        to_tokens.out[...] = side_by_side(context)
        to_tokens.start()
        run(up, "g2")
        if l + 1 < LAYERS:
            run(parts[l + 1], "g1")
        run([proj], "g3")
        to_tokens.wait()
        context = join_context(to_tokens.into)
        first = hidden + nn(context, proj.value()) + small[l, 2:3, :]
        middle, unit, scale = norm_forward(first, small[l, 4:5, :], small[l, 6:7, :])
        unit1[...], scale1[...] = unit, scale
        mid_low = middle.astype(BF16)
        mid_ref[...] = mid_low
        run(up, "g3")
        run(down, "g2")
        for j in range(4):
            at = j * 512
            weight = up[j // 2].full[:, :, :, :, (j % 2) * 512 : (j % 2) * 512 + 512].reshape(D, 512)
            upper = nn(mid_low, weight) + small_up[l, :, at : at + 512]
            phi = 0.5 + 0.5 * lax.erf(upper * (0.5**0.5))
            act_ref[:, at : at + 512] = (upper * phi).astype(BF16)
            density = jnp.exp(-0.5 * upper * upper) * 0.3989422804014327
            slope_ref[:, at : at + 512] = phi + upper * density
        if l + 1 < LAYERS:
            run(parts[l + 1][:3], "g2")
        run(down, "g3")
        second = jnp.concatenate([nn(act_ref[...], part.value()) for part in down], axis=1)
        second = middle + second + small[l, 3:4, :]
        hidden, unit, scale = norm_forward(second, small[l, 5:6, :], small[l, 7:8, :])
        unit2[...], scale2[...] = unit, scale
        if l + 1 < LAYERS:
            run(parts[l + 1][:3], "g3")
    out_ref[...] = hidden.astype(BF16)
    out_copy = pltpu.make_async_copy(out_ref, out_hbm, out_sems.at[0])
    out_copy.start()

    grad = cot_ref[...].astype(F32)
    for l in reversed(range(LAYERS)):
        qkv, proj, up, down = parts[l][:3], parts[l][3], parts[l][4:6], parts[l][6:8]
        above = parts[l + 1] if l + 1 < LAYERS else []
        to_heads, to_tokens, d_to_heads, d_to_tokens = swap[l]
        source_ref, unit1, scale1, unit2, scale2, mid_ref, act_ref, slope_ref = saved[l]
        grad_two, d_small[l, 5:6, :], d_small[l, 7:8, :] = norm_backward(
            grad, unit2[...], scale2[...], small[l, 5:6, :]
        )
        low_two = grad_two.astype(BF16)
        d_small[l, 3:4, :] = column_sum(low_two.astype(F32))
        d_uppers = []
        for j in range(4):
            at = j * 512
            d_act = 0.0
            for i in range(2):
                weight = down[i].full[j // 2, (j % 2) * 2 : (j % 2) * 2 + 2].reshape(512, 256)
                d_act = d_act + nt(low_two[:, i * 256 : (i + 1) * 256], weight)
            d_upper = (d_act * slope_ref[:, at : at + 512]).astype(BF16)
            d_small_up[l, :, at : at + 512] = column_sum(d_upper.astype(F32))
            d_uppers.append(d_upper)
        d_upper = jnp.concatenate(d_uppers, axis=1)
        run(above[:3], "e1")
        grad_mid = grad_two
        for i in range(2):
            grad_mid = grad_mid + nt(d_upper[:, i * 1024 : (i + 1) * 1024], up[i].value())
        grad_one, d_small[l, 4:5, :], d_small[l, 6:7, :] = norm_backward(
            grad_mid, unit1[...], scale1[...], small[l, 4:5, :]
        )
        low_one = grad_one.astype(BF16)
        d_small[l, 2:3, :] = column_sum(low_one.astype(F32))
        d_context = nt(low_one, proj.value()).astype(BF16)
        split_context(d_context, d_to_heads.out)
        d_to_heads.start()
        run(down + up + [proj], "sent")
        for i in range(2):
            for j in range(8):
                block = tn(act_ref[:, j * 256 : (j + 1) * 256], low_two[:, i * 256 : (i + 1) * 256])
                down[i].store(j * 256, block)
            down[i].e0()
        for i in range(2):
            for j in range(2):
                block = tn(mid_ref[:, j * 256 : (j + 1) * 256], d_upper[:, i * 1024 : (i + 1) * 1024])
                up[i].store(j * 256, block)
            up[i].e0()
        context = join_context(to_tokens.into)
        for j in range(2):
            proj.store(j * 256, tn(context[:, j * 256 : (j + 1) * 256], low_one))
        proj.e0()
        d_to_heads.wait()
        run(down, "e1")
        queries, keys, values = head_parts(to_heads.into[...])
        query_ref[...] = queries.reshape(NQ, QB, HD)
        dc_ref[...] = one_above_other(d_to_heads.into[...]).reshape(NQ, QB, HD)
        keys_t = keys.T
        dk_ref[...] = jnp.zeros_like(dk_ref)
        dv_ref[...] = jnp.zeros_like(dv_ref)

        def attend_back(i, carry):
            d_ctx = dc_ref[i]
            d_prob = nt(values, d_ctx)
            prob = probs[l][i]
            row = jnp.sum(prob * d_prob, axis=0, keepdims=True)
            d_score = (prob * (d_prob - row)).astype(BF16)
            dv_ref[...] += nn(prob.astype(BF16), d_ctx)
            dk_ref[...] += nn(d_score, query_ref[i])
            dq_ref[i] = (nn(keys_t, d_score) * 0.125).T.astype(BF16)
            return carry

        lax.fori_loop(0, NQ, attend_back, 0)
        both = jnp.concatenate([dq_ref[...].reshape(LENGTH, HD), dk_ref[...].astype(BF16)], axis=1)
        d_to_tokens.out[:, 0:ROWS, :] = both.reshape(GROUP, ROWS, 2 * HD)
        d_to_tokens.out[:, ROWS:96, :] = side_by_side(dv_ref[...].astype(BF16).reshape(GROUP, ROWS, HD))
        d_to_tokens.start()
        run(up + [proj], "e1")
        run(above, "e2")
        run(qkv, "sent")
        d_to_tokens.wait()
        d_joined = join_heads(d_to_tokens.into)
        d_small[l, 1:2, :] = column_sum(d_joined[:, 2 * D :].astype(F32))
        grad = grad_one
        for i in range(3):
            grad = grad + nt(d_joined[:, i * D : (i + 1) * D], qkv[i].value())
        source = source_ref[...]
        for i in range(3):
            qkv[i].store(0, tn(source, d_joined[:, i * D : (i + 1) * D]))
            qkv[i].e0()
    dx_ref[...] = grad
    dx_copy = pltpu.make_async_copy(dx_ref, dx_hbm, out_sems.at[1])
    dx_copy.start()
    qkv, rest, above = parts[0][:3], parts[0][3:], parts[1]
    run(qkv, "e1")
    run(above, "e3")

    small_grad[...] = jnp.zeros_like(small_grad)
    for l in range(LAYERS):
        for t in range(GROUP):
            small_grad[t, l * 8 + 1 : l * 8 + 8, 0:32] = d_small[l, 1:8, t * 32 : (t + 1) * 32]
            small_grad[t, l * 8 : l * 8 + 1, :] = d_small_up[l, :, t * 128 : (t + 1) * 128]
    for to in p.group():
        remote(small_grad.at[to], small_in.at[me], small_sems.at[2], small_sems.at[3], (p.rep, to))
    small_in[me] = small_grad[me]
    run(rest, "e2")
    run(qkv, "e2")
    run(above, "e4")
    wait_bytes(small_in.at[pl.ds(0, GROUP - 1)], small_sems.at[3])
    total = small_in[0]
    for t in range(1, GROUP):
        total = total + small_in[t]
    slot = small_rep.at[p.rep]
    slot[...] = total
    nrep = nx * nzl
    for d in range(1, nrep):
        remote(slot, slot, small_sems.at[4], small_sems.at[5], (lax.rem(p.rep + d, nrep), me))
    run(rest, "e3")
    run(qkv, "e3")
    run(rest, "e4")
    if nrep > 1:
        wait_bytes(small_rep.at[pl.ds(0, nrep - 1)], small_sems.at[5])
    total = small_rep[0]
    for t in range(1, nrep):
        total = total + small_rep[t]
    for l in range(LAYERS):
        at = l * 8
        upb_out[l : l + 1, :] = total[at : at + 1, :]
        bias_out[l] = total[at + 1 : at + 4, 0:32]
        gain_out[l] = total[at + 4 : at + 6, 0:32]
        shift_out[l] = total[at + 6 : at + 8, 0:32]
    run(qkv, "e4")

    run(everything, "reduced")
    for l in range(LAYERS):
        for one in swap[l]:
            one.finish()
    wait_bytes(small_all.at[pl.ds(0, GROUP - 1)], small_sems.at[0])
    wait_bytes(small_grad.at[pl.ds(0, GROUP - 1)], small_sems.at[2])
    if nrep > 1:
        wait_bytes(small_rep.at[pl.ds(0, nrep - 1)], small_sems.at[4])
    out_copy.wait()
    dx_copy.wait()


def scratch(nx, nzl, members):
    sizes = {"x": nx, "y": Y, "z": ZH * nzl}
    nrep = nx * nzl
    shapes = [pltpu.VMEM((TOK, D), BF16), pltpu.VMEM((TOK, D), F32)]
    shapes += [pltpu.VMEM(member.shape, F32) for member in members[:4]]
    for _ in range(LAYERS):
        for _, _, r, c, _, _ in PARTS:
            shapes.append(pltpu.VMEM((ZH, Y, CORES, r, c), BF16))
    for _ in range(LAYERS):
        for _, _, r, c, _, near in PARTS:
            piece = (r // nrep, c) if r == 128 else (r // nzl, c // nx)
            na, nb, nc = [sizes[axis] for axis in {"x": "xyz", "y": "yxz", "z": "zxy"}[near]]
            shapes.append(pltpu.VMEM((ZH, Y, r, c), BF16))
            shapes.append(pltpu.VMEM((na, nb, nc) + piece, BF16))
            shapes.append(pltpu.VMEM((max(na - 1, 1), nb, nc) + piece, BF16))
            shapes.append(pltpu.VMEM((nb, nc) + piece, BF16))
            shapes.append(pltpu.VMEM((nb * nc - 1,) + piece, BF16))
            shapes.append(pltpu.VMEM((nrep,) + piece, BF16))
    for _ in range(LAYERS):
        for rows in (96, 32, 32, 96):
            shapes += [pltpu.VMEM((GROUP, rows, 128), BF16)] * 2
    shapes += [pltpu.VMEM((16, 128), F32)]
    shapes += [pltpu.VMEM((GROUP, 16, 128), F32)] * 3
    shapes += [pltpu.VMEM((nrep, 16, 128), F32)]
    shapes += [pltpu.VMEM((LAYERS, 8, D), F32), pltpu.VMEM((LAYERS, 1, FF), F32)] * 2
    for _ in range(LAYERS):
        shapes += [
            pltpu.VMEM((TOK, D), BF16),
            pltpu.VMEM((TOK, D), F32),
            pltpu.VMEM((TOK, 1), F32),
            pltpu.VMEM((TOK, D), F32),
            pltpu.VMEM((TOK, 1), F32),
            pltpu.VMEM((TOK, D), BF16),
            pltpu.VMEM((TOK, FF), BF16),
            pltpu.VMEM((TOK, FF), F32),
        ]
    shapes += [pltpu.VMEM((NQ, LENGTH, QB), F32)] * LAYERS
    shapes += [pltpu.VMEM((NQ, QB, HD), BF16)] * 4
    shapes += [pltpu.VMEM((LENGTH, HD), F32)] * 2
    shapes += [
        pltpu.SemaphoreType.DMA((LAYERS * len(PARTS), SEMS)),
        pltpu.SemaphoreType.DMA((LAYERS * 4, 2)),
        pltpu.SemaphoreType.DMA((6,)),
        pltpu.SemaphoreType.DMA((2,)),
    ]
    return shapes


def copy_kernel(*refs):
    n = 10
    source, target, held, sems = refs[:n], refs[n : 2 * n], refs[2 * n : 3 * n], refs[-1]
    into = [pltpu.make_async_copy(source[i], held[i], sems.at[0, i]) for i in range(n)]
    outof = [pltpu.make_async_copy(held[i], target[i], sems.at[1, i]) for i in range(n)]
    for copy in into:
        copy.start()
    for i in range(n):
        into[i].wait()
        outof[i].start()
    for copy in outof:
        copy.wait()


def local_call(nx, nzl, inputs, *arguments):
    cotangent, members = arguments[-1], arguments[:-1]
    shapes = [jax.ShapeDtypeStruct((TOK, D), BF16), jax.ShapeDtypeStruct((TOK, D), F32)]
    shapes += [jax.ShapeDtypeStruct(member.shape, F32) for member in members]
    anywhere, vmem = pl.BlockSpec(memory_space=pl.ANY), pl.BlockSpec(memory_space=pltpu.VMEM)
    got = pl.pallas_call(
        functools.partial(kernel, nx, nzl),
        out_shape=shapes,
        in_specs=[vmem] * 10,
        out_specs=[anywhere] * 6 + [vmem] * 4,
        scratch_shapes=scratch(nx, nzl, members),
        compiler_params=pltpu.CompilerParams(
            collective_id=0, has_side_effects=True, vmem_limit_bytes=63 * 1024 * 1024
        ),
        cost_estimate=pl.CostEstimate(flops=7 * 10**9, bytes_accessed=8 * 10**6, transcendentals=5 * 10**6),
    )(inputs.reshape(TOK, D), cotangent.reshape(TOK, D), *members)
    return pl.pallas_call(
        copy_kernel,
        out_shape=shapes,
        in_specs=[anywhere] * 10,
        out_specs=[anywhere] * 10,
        scratch_shapes=[pltpu.VMEM(shape.shape, shape.dtype) for shape in shapes] + [pltpu.SemaphoreType.DMA((2, 10))],
    )(*got)


def solution(mesh):
    nrep = mesh.shape["rep"]
    nzl = 2 if nrep >= 2 else 1
    nx = nrep // nzl

    def shards(inputs, *arguments):
        got = local_call(nx, nzl, inputs, *arguments)
        return (got[0].reshape(inputs.shape), got[1].reshape(inputs.shape), *got[2:])

    rows, columns = P(None, "shard", None), P(None, None, "shard")
    both = P("rep", "shard", None)
    weights = (rows, rows, rows, rows, columns, columns, columns, P(None, "shard"))
    return jax.shard_map(
        shards,
        mesh=mesh,
        in_specs=(both, *weights, both),
        out_specs=(both, both, *weights),
        check_vma=False,
    )
```

time: 233 us -> 164 us (0.70)
  Pallas kernels: 221 us -> 161 us
  local copies, waits for them, and re-layouts: 10.5 us -> 2.5 us
    pallas_call x1 -> x2, Pallas kernels: 221 us -> 161 us  [the longest x1 158 us: local_call(): pl.pallas_call(functools.partial(kernel, nx, nzl), out_shape=shapes, in_s...]
    unnamed x29 -> x6, local copies, waits for them, and re-layouts: 10.5 us -> 2.5 us
where the time goes in v2:
time: 164 us
  Pallas kernels  161 us (98%)
  local copies, waits for them, and re-layouts  2.5 us (2%)
    pallas_call x1, Pallas kernels, local_call(): pl.pallas_call(functools.partial(kernel, nx, nzl), out_shape=shapes, in_s...  158 us

profile of v2, /device:TPU:0, one launch (start us, length us, event | category | flops | bytes accessed | tf_op | source)
XLA Modules:
  0.0 164.2 jit_solution(10940802982574794713)
XLA Ops:
  0.6 0.0 copy-start.1
  0.7 0.7 copy-done.1
  1.3 0.6 copy.20.refs_6_
  1.9 158.5 %shard_map.177 = (bf16[128,512]{1,0:T(8,128)(2,1)}, f32[128,512]{1,0:T(8,128)}, f32[2,32,1536]{2,1,0:T(8,128)}, f32[2,32,512]{2,1,0:T(8,128)}, f32[2,32,2048]{2,...) custom-call(bf16[128,512]{1,0:T(8,128)(2,1)} %bitcast.5, ...), custom_call_target="tpu_custom_call" | custom-call | flops 7000000000 | bytes 8000000 | tf_op jit(solution)/shard_map/pallas_call | solution.py:768
  160.4 2.5 %shard_map.178 = (bf16[128,512]{1,0:T(8,128)(2,1)}, f32[128,512]{1,0:T(8,128)}, f32[2,32,1536]{2,1,0:T(8,128)}, f32[2,32,512]{2,1,0:T(8,128)}, f32[2,32,2048]{2,...) custom-call(bf16[128,512]{1,0:T(8,128)(2,1)} %get-tuple-element.30.r, ...), custom_call_target="tpu_custom_call" | custom-call | tf_op jit(solution)/shard_map/pallas_call | solution.py:779
  162.9 0.0 copy-start
  162.9 0.7 copy-done
  163.6 0.6 copy.21
Async XLA Ops:
  0.6 0.7 copy-start.1
  162.9 0.7 copy-start

commit v3 on v2

--- a/solution.py
+++ b/solution.py
@@ -20,14 +20,14 @@
 NQ = LENGTH // QB
 QKV, PROJ, UP, DOWN = range(4)
 PARTS = (
-    (QKV, 0, 32, 512, "x", "x"),
-    (QKV, 512, 32, 512, "z", "y"),
-    (QKV, 1024, 32, 512, "y", "x"),
-    (PROJ, 0, 32, 512, "x", "y"),
-    (UP, 0, 32, 1024, "x", "x"),
-    (UP, 1024, 32, 1024, "z", "y"),
-    (DOWN, 0, 128, 256, "x", "x"),
-    (DOWN, 256, 128, 256, "y", "y"),
+    (QKV, 0, 32, 512, "xx", "xx"),
+    (QKV, 512, 32, 512, "zz", "zz"),
+    (QKV, 1024, 32, 512, "yy", "yy"),
+    (PROJ, 0, 32, 512, "xx", "xx"),
+    (UP, 0, 32, 1024, "xx", "xx"),
+    (UP, 1024, 32, 1024, "zz", "zz"),
+    (DOWN, 0, 128, 256, "xx", "xx"),
+    (DOWN, 256, 128, 256, "yz", "yy"),
 )
 SEMS = 17
 
@@ -114,6 +114,9 @@
         for dx in range(1, self.nx):
             for dz in range(self.nz):
                 found.append(self.at(x=self.xs(dx), z=self.zs(dz)))
+        for dx in range(1, self.nx):
+            for dy in range(1, Y):
+                found.append(self.at(x=self.xs(dx), y=self.ys(dy)))
         for dy in range(Y):
             for zh in range(ZH):
                 z = lax.rem(self.z + zh * self.nzl, self.nz)
@@ -137,6 +140,21 @@
             remote(self.out.at[to], self.into.at[me], self.sems.at[0], self.sems.at[1], (self.place.rep, to))
         self.into[me] = self.out[me]
 
+    def send(self, first, blocks):
+        me = self.place.shard
+        for j in range(blocks.shape[0]):
+            self.out[first + j] = blocks[j]
+        for j in range(blocks.shape[0]):
+            to = first + j
+
+            @pl.when(to != me)
+            def _():
+                remote(self.out.at[to], self.into.at[me], self.sems.at[0], self.sems.at[1], (self.place.rep, to))
+
+            @pl.when(to == me)
+            def _():
+                self.into[me] = self.out[me]
+
     def wait(self):
         wait_bytes(self.into.at[pl.ds(0, GROUP - 1)], self.sems.at[1])
 
@@ -145,8 +163,8 @@
 
 
 class Part:
-    def __init__(self, place, own, full, sems, sums, far, near, result, out):
-        self.place, self.own, self.full, self.sems = place, own, full, sems
+    def __init__(self, place, own, full, grad, sems, sums, far, near, result, out):
+        self.place, self.own, self.full, self.grad, self.sems = place, own, full, grad, sems
         self.pair, self.chip, self.recv1, self.sum1, self.recv2, self.recv3 = sums
         self.far, self.near, self.result, self.out = far, near, result, out
         self.rows, self.cols = own.shape
@@ -249,13 +267,13 @@
         per_y = CORES * self.rows
         block = block.astype(BF16)
         if count == ZH * Y * per_y:
-            self.full[...] = block.reshape(ZH, Y, CORES, self.rows, self.cols)
+            self.grad[...] = block.reshape(ZH, Y, CORES, self.rows, self.cols)
         elif count == Y * per_y:
-            self.full[start // count] = block.reshape(Y, CORES, self.rows, self.cols)
+            self.grad[start // count] = block.reshape(Y, CORES, self.rows, self.cols)
         else:
             n = count // per_y
             zh, y = divmod(start // per_y, Y)
-            self.full[zh, y : y + n] = block.reshape(n, CORES, self.rows, self.cols)
+            self.grad[zh, y : y + n] = block.reshape(n, CORES, self.rows, self.cols)
 
     def piece(self, zl, x):
         p = self.place
@@ -267,15 +285,15 @@
         return slice(zl * half, (zl + 1) * half), slice(x * part, (x + 1) * part)
 
     def e0(self):
-        p, full = self.place, self.full
-        remote(full.at[:, :, 1 - p.core], self.pair, self.sem(8), self.sem(9), self.sibling())
+        p = self.place
+        remote(self.grad.at[:, :, 1 - p.core], self.pair, self.sem(8), self.sem(9), self.sibling())
 
     def e1(self):
         p = self.place
         wait_bytes(self.pair, self.sem(9))
         for zh in range(ZH):
             for y in range(Y):
-                total = self.full[zh, y, p.core].astype(F32) + self.pair[zh, y].astype(F32)
+                total = self.grad[zh, y, p.core].astype(F32) + self.pair[zh, y].astype(F32)
                 total = total.astype(BF16)
                 for x in range(p.nx):
                     for zl in range(p.nzl):
@@ -417,13 +435,15 @@
     out_ref, dx_ref = take(2)
     results = take(4)
     full = [take(len(PARTS)) for _ in range(LAYERS)]
+    last_grads = take(3)
     sums = [[take(6) for _ in PARTS] for _ in range(LAYERS)]
     swaps = [take(8) for _ in range(LAYERS)]
     small_own, small_all, small_grad, small_in, small_rep = take(5)
     small, small_up, d_small, d_small_up = take(4)
     saved = [take(8) for _ in range(LAYERS)]
     probs = take(LAYERS)
-    query_ref, dc_ref, ctx_ref, dq_ref, dk_ref, dv_ref = take(6)
+    (shares,) = take(1)
+    query_ref, dc_ref, dq_ref, dk_ref, dv_ref = take(5)
     part_sems, swap_sems, small_sems, out_sems = take(4)
 
     p = Place(nx, nzl)
@@ -437,10 +457,11 @@
                     p,
                     own[w].at[l, :, here],
                     full[l][i],
+                    last_grads[i] if l == 0 and i < 3 else full[l][i],
                     part_sems.at[l * len(PARTS) + i],
                     sums[l][i],
-                    far,
-                    near,
+                    far[l],
+                    near[l],
                     results[w].at[l, :, here],
                     result_hbm[w].at[l, :, here],
                 )
@@ -470,6 +491,12 @@
 
     me = p.shard
 
+    def along(which, axes):
+        return [part for part in which if part.far in axes]
+
+    def first_along(which, axes):
+        return [part for part in which if part.near in axes]
+
     def run(which, *steps):
         for step in steps:
             for part in which:
@@ -477,11 +504,12 @@
 
     early, late = parts[0][:3], parts[0][3:]
     run(early, "g0")
+    run(early, "g1")
     for to in p.group():
         remote(small_own, small_all.at[me], small_sems.at[0], small_sems.at[1], (p.rep, to))
-    run(late, "g0")
-    run(early, "g1")
-    run(late, "g1")
+    run(along(late, "x"), "g0")
+    run(along(late, "yz"), "g0")
+    run(early, "g2")
     wait_bytes(small_all.at[pl.ds(0, GROUP - 1)], small_sems.at[1])
     for l in range(LAYERS):
         for q in range(4):
@@ -489,7 +517,7 @@
             small[l, :, q * 128 : (q + 1) * 128] = jnp.concatenate(part, axis=1)
         for t in range(GROUP):
             small_up[l, :, t * 128 : (t + 1) * 128] = small_all[t, l * 8 : l * 8 + 1, :]
-    run(early, "g2", "g3")
+    run(early, "g3")
 
     hidden = x_ref[...].astype(F32)
     for l in range(LAYERS):
@@ -503,7 +531,10 @@
         split_heads(jnp.concatenate(joined, axis=1).astype(BF16), to_heads.out)
         to_heads.start()
         if l + 1 < LAYERS:
-            run(parts[l + 1], "g0")
+            run(along(late, "x"), "g1")
+        run(up[1:] + down[1:], "g1")
+        if l + 1 < LAYERS:
+            run(parts[l + 1][:3], "g0")
         run([proj], "g2")
         to_heads.wait()
         queries, keys, values = head_parts(to_heads.into[...])
@@ -513,19 +544,20 @@
         def attend(i, carry):
             scores = nt(keys, query_ref[i])
             expo = jnp.exp(scores - jnp.max(scores, axis=0, keepdims=True))
-            prob = expo * (1.0 / jnp.sum(expo, axis=0, keepdims=True))
-            probs[l][i] = prob
-            ctx_ref[i] = nn(values_t, prob.astype(BF16)).T.astype(BF16)
+            part = 1.0 / jnp.sum(expo, axis=0, keepdims=True)
+            low = expo.astype(BF16)
+            probs[l][i] = low
+            shares[l, i] = part
+            block = (nn(values_t, low) * part).T.astype(BF16).reshape(QB // ROWS, ROWS, HD)
+            to_tokens.send(i * (QB // ROWS), side_by_side(block))
             return carry
 
-        lax.fori_loop(0, NQ, attend, 0)
-        context = ctx_ref[...].reshape(GROUP, ROWS, HD)
-        to_tokens.out[...] = side_by_side(context)
-        to_tokens.start()
+        lax.fori_loop(0, NQ, lambda i, carry: attend(lax.rem(i + (1 - p.zh) * (NQ // 2), NQ), carry), 0)
+        if l + 1 < LAYERS:
+            run(parts[l + 1][:3], "g1")
+            run(parts[l + 1][3:], "g0")
+        run([proj], "g3")
         run(up, "g2")
-        if l + 1 < LAYERS:
-            run(parts[l + 1], "g1")
-        run([proj], "g3")
         to_tokens.wait()
         context = join_context(to_tokens.into)
         first = hidden + nn(context, proj.value()) + small[l, 2:3, :]
@@ -543,14 +575,14 @@
             act_ref[:, at : at + 512] = (upper * phi).astype(BF16)
             density = jnp.exp(-0.5 * upper * upper) * 0.3989422804014327
             slope_ref[:, at : at + 512] = phi + upper * density
-        if l + 1 < LAYERS:
-            run(parts[l + 1][:3], "g2")
         run(down, "g3")
         second = jnp.concatenate([nn(act_ref[...], part.value()) for part in down], axis=1)
         second = middle + second + small[l, 3:4, :]
         hidden, unit, scale = norm_forward(second, small[l, 5:6, :], small[l, 7:8, :])
         unit2[...], scale2[...] = unit, scale
         if l + 1 < LAYERS:
+            run(parts[l + 1][:3], "g2")
+            run(along(parts[l + 1][3:], "x"), "g1")
             run(parts[l + 1][:3], "g3")
     out_ref[...] = hidden.astype(BF16)
     out_copy = pltpu.make_async_copy(out_ref, out_hbm, out_sems.at[0])
@@ -578,7 +610,6 @@
             d_small_up[l, :, at : at + 512] = column_sum(d_upper.astype(F32))
             d_uppers.append(d_upper)
         d_upper = jnp.concatenate(d_uppers, axis=1)
-        run(above[:3], "e1")
         grad_mid = grad_two
         for i in range(2):
             grad_mid = grad_mid + nt(d_upper[:, i * 1024 : (i + 1) * 1024], up[i].value())
@@ -591,22 +622,29 @@
         split_context(d_context, d_to_heads.out)
         d_to_heads.start()
         run(down + up + [proj], "sent")
-        for i in range(2):
+
+        def down_grad(i):
             for j in range(8):
                 block = tn(act_ref[:, j * 256 : (j + 1) * 256], low_two[:, i * 256 : (i + 1) * 256])
                 down[i].store(j * 256, block)
             down[i].e0()
-        for i in range(2):
+
+        def up_grad(i):
             for j in range(2):
                 block = tn(mid_ref[:, j * 256 : (j + 1) * 256], d_upper[:, i * 1024 : (i + 1) * 1024])
                 up[i].store(j * 256, block)
             up[i].e0()
+
+        down_grad(0)
+        up_grad(0)
+        run(above[:3], "e1")
         context = join_context(to_tokens.into)
         for j in range(2):
             proj.store(j * 256, tn(context[:, j * 256 : (j + 1) * 256], low_one))
         proj.e0()
+        run(above[3:], "e2")
+        run(first_along(down + up + [proj], "x"), "e1")
         d_to_heads.wait()
-        run(down, "e1")
         queries, keys, values = head_parts(to_heads.into[...])
         query_ref[...] = queries.reshape(NQ, QB, HD)
         dc_ref[...] = one_above_other(d_to_heads.into[...]).reshape(NQ, QB, HD)
@@ -617,7 +655,7 @@
         def attend_back(i, carry):
             d_ctx = dc_ref[i]
             d_prob = nt(values, d_ctx)
-            prob = probs[l][i]
+            prob = probs[l][i].astype(F32) * shares[l, i]
             row = jnp.sum(prob * d_prob, axis=0, keepdims=True)
             d_score = (prob * (d_prob - row)).astype(BF16)
             dv_ref[...] += nn(prob.astype(BF16), d_ctx)
@@ -630,25 +668,32 @@
         d_to_tokens.out[:, 0:ROWS, :] = both.reshape(GROUP, ROWS, 2 * HD)
         d_to_tokens.out[:, ROWS:96, :] = side_by_side(dv_ref[...].astype(BF16).reshape(GROUP, ROWS, HD))
         d_to_tokens.start()
-        run(up + [proj], "e1")
-        run(above, "e2")
+        down_grad(1)
+        up_grad(1)
+        run(above[:3], "e2")
+        run(first_along(down + up + [proj], "yz"), "e1")
         run(qkv, "sent")
+        run(first_along(above[3:], "x"), "e3")
         d_to_tokens.wait()
         d_joined = join_heads(d_to_tokens.into)
         d_small[l, 1:2, :] = column_sum(d_joined[:, 2 * D :].astype(F32))
         grad = grad_one
+        source = source_ref[...]
+        if l == 0:
+            for i in range(3):
+                qkv[i].store(0, tn(source, d_joined[:, i * D : (i + 1) * D]))
+                qkv[i].e0()
         for i in range(3):
             grad = grad + nt(d_joined[:, i * D : (i + 1) * D], qkv[i].value())
-        source = source_ref[...]
-        for i in range(3):
-            qkv[i].store(0, tn(source, d_joined[:, i * D : (i + 1) * D]))
-            qkv[i].e0()
+        if l > 0:
+            for i in range(3):
+                qkv[i].store(0, tn(source, d_joined[:, i * D : (i + 1) * D]))
+                qkv[i].e0()
     dx_ref[...] = grad
     dx_copy = pltpu.make_async_copy(dx_ref, dx_hbm, out_sems.at[1])
     dx_copy.start()
     qkv, rest, above = parts[0][:3], parts[0][3:], parts[1]
     run(qkv, "e1")
-    run(above, "e3")
 
     small_grad[...] = jnp.zeros_like(small_grad)
     for l in range(LAYERS):
@@ -658,9 +703,11 @@
     for to in p.group():
         remote(small_grad.at[to], small_in.at[me], small_sems.at[2], small_sems.at[3], (p.rep, to))
     small_in[me] = small_grad[me]
-    run(rest, "e2")
+    run(first_along(rest, "x"), "e2")
+    run(first_along(above[3:], "yz") + above[:3], "e3")
+    run(first_along(rest, "yz"), "e2")
     run(qkv, "e2")
-    run(above, "e4")
+    run(rest, "e3")
     wait_bytes(small_in.at[pl.ds(0, GROUP - 1)], small_sems.at[3])
     total = small_in[0]
     for t in range(1, GROUP):
@@ -670,7 +717,7 @@
     nrep = nx * nzl
     for d in range(1, nrep):
         remote(slot, slot, small_sems.at[4], small_sems.at[5], (lax.rem(p.rep + d, nrep), me))
-    run(rest, "e3")
+    run(above, "e4")
     run(qkv, "e3")
     run(rest, "e4")
     if nrep > 1:
@@ -706,10 +753,12 @@
     for _ in range(LAYERS):
         for _, _, r, c, _, _ in PARTS:
             shapes.append(pltpu.VMEM((ZH, Y, CORES, r, c), BF16))
-    for _ in range(LAYERS):
+    for _, _, r, c, _, _ in PARTS[:3]:
+        shapes.append(pltpu.VMEM((ZH, Y, CORES, r, c), BF16))
+    for l in range(LAYERS):
         for _, _, r, c, _, near in PARTS:
             piece = (r // nrep, c) if r == 128 else (r // nzl, c // nx)
-            na, nb, nc = [sizes[axis] for axis in {"x": "xyz", "y": "yxz", "z": "zxy"}[near]]
+            na, nb, nc = [sizes[axis] for axis in {"x": "xyz", "y": "yxz", "z": "zxy"}[near[l]]]
             shapes.append(pltpu.VMEM((ZH, Y, r, c), BF16))
             shapes.append(pltpu.VMEM((na, nb, nc) + piece, BF16))
             shapes.append(pltpu.VMEM((max(na - 1, 1), nb, nc) + piece, BF16))
@@ -734,8 +783,9 @@
             pltpu.VMEM((TOK, FF), BF16),
             pltpu.VMEM((TOK, FF), F32),
         ]
-    shapes += [pltpu.VMEM((NQ, LENGTH, QB), F32)] * LAYERS
-    shapes += [pltpu.VMEM((NQ, QB, HD), BF16)] * 4
+    shapes += [pltpu.VMEM((NQ, LENGTH, QB), BF16)] * LAYERS
+    shapes += [pltpu.VMEM((LAYERS, NQ, 1, QB), F32)]
+    shapes += [pltpu.VMEM((NQ, QB, HD), BF16)] * 3
     shapes += [pltpu.VMEM((LENGTH, HD), F32)] * 2
     shapes += [
         pltpu.SemaphoreType.DMA((LAYERS * len(PARTS), SEMS)),

time: 164 us -> 149 us (0.909)
  Pallas kernels: 161 us -> 146 us
    pallas_call x1, Pallas kernels: 158 us -> 143 us  [local_call(): pl.pallas_call(functools.partial(kernel, nx, nzl), out_shape=shapes, in_s...]
where the time goes in v3:
time: 149 us
  Pallas kernels  146 us (98%)
  local copies, waits for them, and re-layouts  2.5 us (2%)
    pallas_call x1, Pallas kernels, local_call(): pl.pallas_call(functools.partial(kernel, nx, nzl), out_shape=shapes, in_s...  143 us

profile of v3, /device:TPU:0, one launch (start us, length us, event | category | flops | bytes accessed | tf_op | source)
XLA Modules:
  0.0 148.9 jit_solution(4953904220023300146)
XLA Ops:
  0.6 0.0 copy-start.1
  0.7 0.7 copy-done.1
  1.3 0.6 copy.20.refs_6_
  1.9 143.2 %shard_map.177 = (bf16[128,512]{1,0:T(8,128)(2,1)}, f32[128,512]{1,0:T(8,128)}, f32[2,32,1536]{2,1,0:T(8,128)}, f32[2,32,512]{2,1,0:T(8,128)}, f32[2,32,2048]{2,...) custom-call(bf16[128,512]{1,0:T(8,128)(2,1)} %bitcast.5, ...), custom_call_target="tpu_custom_call" | custom-call | flops 7000000000 | bytes 8000000 | tf_op jit(solution)/shard_map/pallas_call | solution.py:818
  145.1 2.5 %shard_map.178 = (bf16[128,512]{1,0:T(8,128)(2,1)}, f32[128,512]{1,0:T(8,128)}, f32[2,32,1536]{2,1,0:T(8,128)}, f32[2,32,512]{2,1,0:T(8,128)}, f32[2,32,2048]{2,...) custom-call(bf16[128,512]{1,0:T(8,128)(2,1)} %get-tuple-element.30.r, ...), custom_call_target="tpu_custom_call" | custom-call | tf_op jit(solution)/shard_map/pallas_call | solution.py:829
  147.6 0.0 copy-start
  147.6 0.7 copy-done
  148.3 0.6 copy.21
Async XLA Ops:
  0.6 0.7 copy-start.1
  147.6 0.7 copy-start

commit v4 on v3

--- a/solution.py
+++ b/solution.py
@@ -16,8 +16,9 @@
 ROWS = 64
 TOK = 2 * ROWS
 LENGTH = GROUP * ROWS
-QB = 256
+QB = 512
 NQ = LENGTH // QB
+UNROLL = NQ // ZH
 QKV, PROJ, UP, DOWN = range(4)
 PARTS = (
     (QKV, 0, 32, 512, "xx", "xx"),
@@ -27,9 +28,20 @@
     (UP, 0, 32, 1024, "xx", "xx"),
     (UP, 1024, 32, 1024, "zz", "zz"),
     (DOWN, 0, 128, 256, "xx", "xx"),
-    (DOWN, 256, 128, 256, "yz", "yy"),
+    (DOWN, 256, 128, 256, "yy", "yy"),
 )
 SEMS = 17
+AXES = {"x": "xyz", "y": "yxz", "z": "zxy"}
+
+
+def piece_shape(rows, cols, nx, nzl):
+    return (rows // (nx * nzl), cols) if rows == 128 else (rows // nzl, cols // nx)
+
+
+def bundles(nx, nzl):
+    if nx * nzl == 8:
+        return ((0,), (1,), (2,), (3, 4, 6), (5,), (7,))
+    return tuple((i,) for i in (0, 1, 2, 3, 4, 6, 5, 7))
 
 
 def nn(a, b):
@@ -163,15 +175,10 @@
 
 
 class Part:
-    def __init__(self, place, own, full, grad, sems, sums, far, near, result, out):
+    def __init__(self, place, own, full, grad, sems, pair, far, near, result, out):
         self.place, self.own, self.full, self.grad, self.sems = place, own, full, grad, sems
-        self.pair, self.chip, self.recv1, self.sum1, self.recv2, self.recv3 = sums
-        self.far, self.near, self.result, self.out = far, near, result, out
+        self.pair, self.far, self.near, self.result, self.out = pair, far, near, result, out
         self.rows, self.cols = own.shape
-        p = place
-        self.n = {"x": p.nx, "y": Y, "z": p.nz}
-        self.me = {"x": p.x, "y": p.y, "z": p.z}
-        self.axes = {"x": "xyz", "y": "yxz", "z": "zxy"}[near]
 
     def sem(self, i):
         return self.sems.at[i]
@@ -288,18 +295,40 @@
         p = self.place
         remote(self.grad.at[:, :, 1 - p.core], self.pair, self.sem(8), self.sem(9), self.sibling())
 
+
+class Sum:
+    def __init__(self, place, parts, buffers):
+        self.place, self.parts, self.sems = place, parts, parts[0].sems
+        self.chip, self.recv1, self.sum1, self.recv2, self.recv3 = buffers
+        p = place
+        self.n = {"x": p.nx, "y": Y, "z": p.nz}
+        self.me = {"x": p.x, "y": p.y, "z": p.z}
+        self.axes = AXES[parts[0].near]
+
+    def sem(self, i):
+        return self.sems.at[i]
+
+    def columns(self):
+        at = 0
+        for part in self.parts:
+            rows, cols = piece_shape(part.rows, part.cols, self.place.nx, self.place.nzl)
+            yield part, slice(at, at + cols)
+            at += cols
+
     def e1(self):
         p = self.place
-        wait_bytes(self.pair, self.sem(9))
-        for zh in range(ZH):
-            for y in range(Y):
-                total = self.grad[zh, y, p.core].astype(F32) + self.pair[zh, y].astype(F32)
-                total = total.astype(BF16)
-                for x in range(p.nx):
-                    for zl in range(p.nzl):
-                        at = {"x": x, "y": y, "z": zh * p.nzl + zl}
-                        rows, cols = self.piece(zl, x)
-                        self.chip[tuple(at[axis] for axis in self.axes)] = total[rows, cols]
+        for part, here in self.columns():
+            wait_bytes(part.pair, part.sem(9))
+            for zh in range(ZH):
+                for y in range(Y):
+                    total = part.grad[zh, y, p.core].astype(F32) + part.pair[zh, y].astype(F32)
+                    total = total.astype(BF16)
+                    for x in range(p.nx):
+                        for zl in range(p.nzl):
+                            at = {"x": x, "y": y, "z": zh * p.nzl + zl}
+                            rows, cols = part.piece(zl, x)
+                            a, b, c = [at[axis] for axis in self.axes]
+                            self.chip[a, b, c, :, here] = total[rows, cols]
         a = self.axes[0]
         for d in order_of(self.n[a]):
             to = lax.rem(self.me[a] + d, self.n[a])
@@ -345,21 +374,23 @@
         nrep = p.nx * p.nzl
         if nrep > 1:
             wait_bytes(self.recv3.at[pl.ds(0, nrep - 1)], self.sem(15))
-        for zl in range(p.nzl):
-            for x in range(p.nx):
-                rows, cols = self.piece(zl, x)
-                self.result[rows, cols] = self.recv3[zl * p.nx + x].astype(F32)
-        pltpu.make_async_copy(self.result, self.out, self.sem(16)).start()
+        for part, here in self.columns():
+            for zl in range(p.nzl):
+                for x in range(p.nx):
+                    rows, cols = part.piece(zl, x)
+                    part.result[rows, cols] = self.recv3[zl * p.nx + x, :, here].astype(F32)
+            pltpu.make_async_copy(part.result, part.out, part.sem(16)).start()
 
     def reduced(self):
         p = self.place
-        wait_bytes(self.pair, self.sem(8))
+        for part in self.parts:
+            wait_bytes(part.pair, part.sem(8))
+            pltpu.make_async_copy(part.result, part.out, part.sem(16)).wait()
         if self.n[self.axes[0]] > 1:
             wait_bytes(self.recv1, self.sem(10))
         wait_bytes(self.recv2, self.sem(12))
         if p.nx * p.nzl > 1:
             wait_bytes(self.recv3.at[pl.ds(0, p.nx * p.nzl - 1)], self.sem(14))
-        pltpu.make_async_copy(self.result, self.out, self.sem(16)).wait()
 
 
 def order_of(n):
@@ -436,7 +467,8 @@
     results = take(4)
     full = [take(len(PARTS)) for _ in range(LAYERS)]
     last_grads = take(3)
-    sums = [[take(6) for _ in PARTS] for _ in range(LAYERS)]
+    pairs = [take(len(PARTS)) for _ in range(LAYERS)]
+    buffers = [[take(5) for _ in bundles(nx, nzl)] for _ in range(LAYERS)]
     swaps = [take(8) for _ in range(LAYERS)]
     small_own, small_all, small_grad, small_in, small_rep = take(5)
     small, small_up, d_small, d_small_up = take(4)
@@ -459,7 +491,7 @@
                     full[l][i],
                     last_grads[i] if l == 0 and i < 3 else full[l][i],
                     part_sems.at[l * len(PARTS) + i],
-                    sums[l][i],
+                    pairs[l][i],
                     far[l],
                     near[l],
                     results[w].at[l, :, here],
@@ -472,6 +504,10 @@
         for l in range(LAYERS)
     ]
     everything = [part for row in parts for part in row]
+    sums = [
+        [Sum(p, [parts[l][i] for i in which], buffers[l][k]) for k, which in enumerate(bundles(nx, nzl))]
+        for l in range(LAYERS)
+    ]
 
     for part in everything:
         part.keep()
@@ -495,7 +531,7 @@
         return [part for part in which if part.far in axes]
 
     def first_along(which, axes):
-        return [part for part in which if part.near in axes]
+        return [one for one in which if one.parts[0].near in axes]
 
     def run(which, *steps):
         for step in steps:
@@ -530,8 +566,7 @@
         joined[2] = joined[2] + small[l, 1:2, :]
         split_heads(jnp.concatenate(joined, axis=1).astype(BF16), to_heads.out)
         to_heads.start()
-        if l + 1 < LAYERS:
-            run(along(late, "x"), "g1")
+        run(along(late, "x") if l == 0 else down[:1], "g1")
         run(up[1:] + down[1:], "g1")
         if l + 1 < LAYERS:
             run(parts[l + 1][:3], "g0")
@@ -541,7 +576,7 @@
         query_ref[...] = queries.reshape(NQ, QB, HD)
         values_t = values.T
 
-        def attend(i, carry):
+        def attend(i):
             scores = nt(keys, query_ref[i])
             expo = jnp.exp(scores - jnp.max(scores, axis=0, keepdims=True))
             part = 1.0 / jnp.sum(expo, axis=0, keepdims=True)
@@ -549,10 +584,16 @@
             probs[l][i] = low
             shares[l, i] = part
             block = (nn(values_t, low) * part).T.astype(BF16).reshape(QB // ROWS, ROWS, HD)
-            to_tokens.send(i * (QB // ROWS), side_by_side(block))
+            return side_by_side(block)
+
+        def attend_half(i, carry):
+            first = lax.rem(i + 1 - p.zh, ZH) * UNROLL
+            blocks = [attend(first + j) for j in range(UNROLL)]
+            to_tokens.send(first * (QB // ROWS), jnp.concatenate(blocks, axis=0))
             return carry
 
-        lax.fori_loop(0, NQ, lambda i, carry: attend(lax.rem(i + (1 - p.zh) * (NQ // 2), NQ), carry), 0)
+        for half in range(ZH):
+            attend_half(half, 0)
         if l + 1 < LAYERS:
             run(parts[l + 1][:3], "g1")
             run(parts[l + 1][3:], "g0")
@@ -582,7 +623,7 @@
         unit2[...], scale2[...] = unit, scale
         if l + 1 < LAYERS:
             run(parts[l + 1][:3], "g2")
-            run(along(parts[l + 1][3:], "x"), "g1")
+            run(parts[l + 1][3:5], "g1")
             run(parts[l + 1][:3], "g3")
     out_ref[...] = hidden.astype(BF16)
     out_copy = pltpu.make_async_copy(out_ref, out_hbm, out_sems.at[0])
@@ -591,7 +632,7 @@
     grad = cot_ref[...].astype(F32)
     for l in reversed(range(LAYERS)):
         qkv, proj, up, down = parts[l][:3], parts[l][3], parts[l][4:6], parts[l][6:8]
-        above = parts[l + 1] if l + 1 < LAYERS else []
+        above = sums[l + 1] if l + 1 < LAYERS else []
         to_heads, to_tokens, d_to_heads, d_to_tokens = swap[l]
         source_ref, unit1, scale1, unit2, scale2, mid_ref, act_ref, slope_ref = saved[l]
         grad_two, d_small[l, 5:6, :], d_small[l, 7:8, :] = norm_backward(
@@ -638,40 +679,42 @@
         down_grad(0)
         up_grad(0)
         run(above[:3], "e1")
+        if l == 0:
+            down_grad(1)
+            up_grad(1)
         context = join_context(to_tokens.into)
         for j in range(2):
             proj.store(j * 256, tn(context[:, j * 256 : (j + 1) * 256], low_one))
         proj.e0()
         run(above[3:], "e2")
-        run(first_along(down + up + [proj], "x"), "e1")
+        run(first_along(sums[l][3:], "x"), "e1")
         d_to_heads.wait()
         queries, keys, values = head_parts(to_heads.into[...])
         query_ref[...] = queries.reshape(NQ, QB, HD)
         dc_ref[...] = one_above_other(d_to_heads.into[...]).reshape(NQ, QB, HD)
         keys_t = keys.T
-        dk_ref[...] = jnp.zeros_like(dk_ref)
-        dv_ref[...] = jnp.zeros_like(dv_ref)
-
-        def attend_back(i, carry):
+
+        def attend_back(i):
             d_ctx = dc_ref[i]
             d_prob = nt(values, d_ctx)
             prob = probs[l][i].astype(F32) * shares[l, i]
             row = jnp.sum(prob * d_prob, axis=0, keepdims=True)
             d_score = (prob * (d_prob - row)).astype(BF16)
-            dv_ref[...] += nn(prob.astype(BF16), d_ctx)
-            dk_ref[...] += nn(d_score, query_ref[i])
             dq_ref[i] = (nn(keys_t, d_score) * 0.125).T.astype(BF16)
-            return carry
-
-        lax.fori_loop(0, NQ, attend_back, 0)
+            return nn(prob.astype(BF16), d_ctx), nn(d_score, query_ref[i])
+
+        terms = [attend_back(i) for i in range(NQ)]
+        dv_ref[...] = sum(term[0] for term in terms)
+        dk_ref[...] = sum(term[1] for term in terms)
         both = jnp.concatenate([dq_ref[...].reshape(LENGTH, HD), dk_ref[...].astype(BF16)], axis=1)
         d_to_tokens.out[:, 0:ROWS, :] = both.reshape(GROUP, ROWS, 2 * HD)
         d_to_tokens.out[:, ROWS:96, :] = side_by_side(dv_ref[...].astype(BF16).reshape(GROUP, ROWS, HD))
         d_to_tokens.start()
-        down_grad(1)
-        up_grad(1)
+        if l > 0:
+            down_grad(1)
+            up_grad(1)
         run(above[:3], "e2")
-        run(first_along(down + up + [proj], "yz"), "e1")
+        run(first_along(sums[l][3:], "yz"), "e1")
         run(qkv, "sent")
         run(first_along(above[3:], "x"), "e3")
         d_to_tokens.wait()
@@ -692,7 +735,7 @@
     dx_ref[...] = grad
     dx_copy = pltpu.make_async_copy(dx_ref, dx_hbm, out_sems.at[1])
     dx_copy.start()
-    qkv, rest, above = parts[0][:3], parts[0][3:], parts[1]
+    qkv, rest, above = sums[0][:3], sums[0][3:], sums[1]
     run(qkv, "e1")
 
     small_grad[...] = jnp.zeros_like(small_grad)
@@ -733,7 +776,7 @@
         shift_out[l] = total[at + 6 : at + 8, 0:32]
     run(qkv, "e4")
 
-    run(everything, "reduced")
+    run(sums[0] + sums[1], "reduced")
     for l in range(LAYERS):
         for one in swap[l]:
             one.finish()
@@ -755,11 +798,14 @@
             shapes.append(pltpu.VMEM((ZH, Y, CORES, r, c), BF16))
     for _, _, r, c, _, _ in PARTS[:3]:
         shapes.append(pltpu.VMEM((ZH, Y, CORES, r, c), BF16))
+    for _ in range(LAYERS):
+        for _, _, r, c, _, _ in PARTS:
+            shapes.append(pltpu.VMEM((ZH, Y, r, c), BF16))
     for l in range(LAYERS):
-        for _, _, r, c, _, near in PARTS:
-            piece = (r // nrep, c) if r == 128 else (r // nzl, c // nx)
-            na, nb, nc = [sizes[axis] for axis in {"x": "xyz", "y": "yxz", "z": "zxy"}[near[l]]]
-            shapes.append(pltpu.VMEM((ZH, Y, r, c), BF16))
+        for which in bundles(nx, nzl):
+            pieces = [piece_shape(PARTS[i][2], PARTS[i][3], nx, nzl) for i in which]
+            piece = (pieces[0][0], sum(cols for _, cols in pieces))
+            na, nb, nc = [sizes[axis] for axis in AXES[PARTS[which[0]][5][l]]]
             shapes.append(pltpu.VMEM((na, nb, nc) + piece, BF16))
             shapes.append(pltpu.VMEM((max(na - 1, 1), nb, nc) + piece, BF16))
             shapes.append(pltpu.VMEM((nb, nc) + piece, BF16))

time: 149 us -> 143 us (0.960)
  Pallas kernels: 146 us -> 140 us
    pallas_call x1, Pallas kernels: 143 us -> 137 us  [local_call(): pl.pallas_call(functools.partial(kernel, nx, nzl), out_shape=shapes, in_s...]
where the time goes in v4:
time: 143 us
  Pallas kernels  140 us (98%)
  local copies, waits for them, and re-layouts  2.5 us (2%)
    pallas_call x1, Pallas kernels, local_call(): pl.pallas_call(functools.partial(kernel, nx, nzl), out_shape=shapes, in_s...  137 us

profile of v4, /device:TPU:0, one launch (start us, length us, event | category | flops | bytes accessed | tf_op | source)
XLA Modules:
  0.0 143.1 jit_solution(12328609253093085445)
XLA Ops:
  0.6 0.0 copy-start.1
  0.7 0.7 copy-done.1
  1.3 0.6 copy.20.refs_6_
  1.9 137.4 %shard_map.177 = (bf16[128,512]{1,0:T(8,128)(2,1)}, f32[128,512]{1,0:T(8,128)}, f32[2,32,1536]{2,1,0:T(8,128)}, f32[2,32,512]{2,1,0:T(8,128)}, f32[2,32,2048]{2,...) custom-call(bf16[128,512]{1,0:T(8,128)(2,1)} %bitcast.5, ...), custom_call_target="tpu_custom_call" | custom-call | flops 7000000000 | bytes 8000000 | tf_op jit(solution)/shard_map/pallas_call | solution.py:864
  139.3 2.5 %shard_map.178 = (bf16[128,512]{1,0:T(8,128)(2,1)}, f32[128,512]{1,0:T(8,128)}, f32[2,32,1536]{2,1,0:T(8,128)}, f32[2,32,512]{2,1,0:T(8,128)}, f32[2,32,2048]{2,...) custom-call(bf16[128,512]{1,0:T(8,128)(2,1)} %get-tuple-element.30.r, ...), custom_call_target="tpu_custom_call" | custom-call | tf_op jit(solution)/shard_map/pallas_call | solution.py:875
  141.8 0.0 copy-start
  141.8 0.7 copy-done
  142.5 0.6 copy.21
Async XLA Ops:
  0.6 0.7 copy-start.1
  141.8 0.7 copy-start

commit v5 on v4

--- a/solution.py
+++ b/solution.py
@@ -515,7 +515,8 @@
     for l in range(LAYERS):
         at = l * 8
         small_own[at : at + 1, :] = upb_ref[l : l + 1, :].astype(F32)
-        small_own[at + 1 : at + 4, 0:32] = bias_ref[l].astype(F32)
+        for i in range(3):
+            small_own[at + 1 + i : at + 2 + i, 0:32] = bias_ref[i, l : l + 1, :].astype(F32)
         small_own[at + 4 : at + 6, 0:32] = gain_ref[l].astype(F32)
         small_own[at + 6 : at + 8, 0:32] = shift_ref[l].astype(F32)
     small_all[p.shard] = small_own[...]
@@ -771,7 +772,8 @@
     for l in range(LAYERS):
         at = l * 8
         upb_out[l : l + 1, :] = total[at : at + 1, :]
-        bias_out[l] = total[at + 1 : at + 4, 0:32]
+        for i in range(3):
+            bias_out[i, l : l + 1, :] = total[at + 1 + i : at + 2 + i, 0:32]
         gain_out[l] = total[at + 4 : at + 6, 0:32]
         shift_out[l] = total[at + 6 : at + 8, 0:32]
     run(qkv, "e4")
@@ -857,7 +859,8 @@
 
 
 def local_call(nx, nzl, inputs, *arguments):
-    cotangent, members = arguments[-1], arguments[:-1]
+    cotangent, members = arguments[-1], list(arguments[:-1])
+    members[4] = members[4].transpose(1, 0, 2)
     shapes = [jax.ShapeDtypeStruct((TOK, D), BF16), jax.ShapeDtypeStruct((TOK, D), F32)]
     shapes += [jax.ShapeDtypeStruct(member.shape, F32) for member in members]
     anywhere, vmem = pl.BlockSpec(memory_space=pl.ANY), pl.BlockSpec(memory_space=pltpu.VMEM)
@@ -872,13 +875,14 @@
         ),
         cost_estimate=pl.CostEstimate(flops=7 * 10**9, bytes_accessed=8 * 10**6, transcendentals=5 * 10**6),
     )(inputs.reshape(TOK, D), cotangent.reshape(TOK, D), *members)
-    return pl.pallas_call(
+    got = pl.pallas_call(
         copy_kernel,
         out_shape=shapes,
         in_specs=[anywhere] * 10,
         out_specs=[anywhere] * 10,
         scratch_shapes=[pltpu.VMEM(shape.shape, shape.dtype) for shape in shapes] + [pltpu.SemaphoreType.DMA((2, 10))],
     )(*got)
+    return (*got[:6], got[6].transpose(1, 0, 2), *got[7:])
 
 
 def solution(mesh):

time: 143 us -> 141 us (0.986)
  local copies, waits for them, and re-layouts: 2.5 us -> 0 us
    unnamed x6 -> x0, local copies, waits for them, and re-layouts: 2.5 us -> none
where the time goes in v5:
time: 141 us
  Pallas kernels  140 us (99%)
    pallas_call x1, Pallas kernels, local_call(): pl.pallas_call(functools.partial(kernel, nx, nzl), out_shape=shapes, in_s...  137 us

profile of v5, /device:TPU:0, one launch (start us, length us, event | category | flops | bytes accessed | tf_op | source)
XLA Modules:
  0.0 140.8 jit_solution(1429975343548270850)
XLA Ops:
  0.6 137.4 %shard_map.177 = (bf16[128,512]{1,0:T(8,128)(2,1)}, f32[128,512]{1,0:T(8,128)}, f32[2,32,1536]{2,1,0:T(8,128)}, f32[2,32,512]{2,1,0:T(8,128)}, f32[2,32,2048]{2,...) custom-call(bf16[128,512]{1,0:T(8,128)(2,1)} %bitcast.7, ...), custom_call_target="tpu_custom_call" | custom-call | flops 7000000000 | bytes 8000000 | tf_op jit(solution)/shard_map/pallas_call | solution.py:867
  138.1 2.5 %shard_map.178 = (bf16[128,512]{1,0:T(8,128)(2,1)}, f32[128,512]{1,0:T(8,128)}, f32[2,32,1536]{2,1,0:T(8,128)}, f32[2,32,512]{2,1,0:T(8,128)}, f32[2,32,2048]{2,...) custom-call(bf16[128,512]{1,0:T(8,128)(2,1)} %get-tuple-element.30.r, ...), custom_call_target="tpu_custom_call" | custom-call | tf_op jit(solution)/shard_map/pallas_call | solution.py:878

commit v6 on v5

--- a/solution.py
+++ b/solution.py
@@ -601,6 +601,7 @@
         run([proj], "g3")
         run(up, "g2")
         to_tokens.wait()
+        run(down, "g2")
         context = join_context(to_tokens.into)
         first = hidden + nn(context, proj.value()) + small[l, 2:3, :]
         middle, unit, scale = norm_forward(first, small[l, 4:5, :], small[l, 6:7, :])
@@ -608,7 +609,6 @@
         mid_low = middle.astype(BF16)
         mid_ref[...] = mid_low
         run(up, "g3")
-        run(down, "g2")
         for j in range(4):
             at = j * 512
             weight = up[j // 2].full[:, :, :, :, (j % 2) * 512 : (j % 2) * 512 + 512].reshape(D, 512)
@@ -618,12 +618,13 @@
             density = jnp.exp(-0.5 * upper * upper) * 0.3989422804014327
             slope_ref[:, at : at + 512] = phi + upper * density
         run(down, "g3")
+        if l + 1 < LAYERS:
+            run(parts[l + 1][:3], "g2")
         second = jnp.concatenate([nn(act_ref[...], part.value()) for part in down], axis=1)
         second = middle + second + small[l, 3:4, :]
         hidden, unit, scale = norm_forward(second, small[l, 5:6, :], small[l, 7:8, :])
         unit2[...], scale2[...] = unit, scale
         if l + 1 < LAYERS:
-            run(parts[l + 1][:3], "g2")
             run(parts[l + 1][3:5], "g1")
             run(parts[l + 1][:3], "g3")
     out_ref[...] = hidden.astype(BF16)

time: 141 us -> 141 us (level)
  no operation moved by 1% of the time
where the time goes in v6:
time: 141 us; the launch traced here: 140 us
  Pallas kernels  139 us (99%)
    pallas_call x1, Pallas kernels, local_call(): pl.pallas_call(functools.partial(kernel, nx, nzl), out_shape=shapes, in_s...  137 us

profile of v6, /device:TPU:0, one launch (start us, length us, event | category | flops | bytes accessed | tf_op | source)
XLA Modules:
  0.0 140.3 jit_solution(14236959875326081918)
XLA Ops:
  0.6 136.9 %shard_map.177 = (bf16[128,512]{1,0:T(8,128)(2,1)}, f32[128,512]{1,0:T(8,128)}, f32[2,32,1536]{2,1,0:T(8,128)}, f32[2,32,512]{2,1,0:T(8,128)}, f32[2,32,2048]{2,...) custom-call(bf16[128,512]{1,0:T(8,128)(2,1)} %bitcast.7, ...), custom_call_target="tpu_custom_call" | custom-call | flops 7000000000 | bytes 8000000 | tf_op jit(solution)/shard_map/pallas_call | solution.py:868
  137.6 2.5 %shard_map.178 = (bf16[128,512]{1,0:T(8,128)(2,1)}, f32[128,512]{1,0:T(8,128)}, f32[2,32,1536]{2,1,0:T(8,128)}, f32[2,32,512]{2,1,0:T(8,128)}, f32[2,32,2048]{2,...) custom-call(bf16[128,512]{1,0:T(8,128)(2,1)} %get-tuple-element.30.r, ...), custom_call_target="tpu_custom_call" | custom-call | tf_op jit(solution)/shard_map/pallas_call | solution.py:879
